TPU v7x, 32 devices: a whole 2x2x4 slice. The times are simulated.
32 devices in a mesh: tm: 16 (over z, x, core), chan: 2 (over y).
Axes of the slice: x: 2, y: 2, z: 4, core: 2. Of those that a mesh axis runs over, the one named last changes fastest.
Arguments:
- features: bfloat16 [512, 64, 128], P('chan', 'tm'), may hold values from -6 to 6
- gain_one: float32 [512], replicated, may hold values from 0.1 to 1.9
- shift_one: float32 [512], replicated, may hold values from -3 to 3
- conv_one: bfloat16 [27, 512, 512], P(None, None, 'chan'), may hold values from -0.0546875 to 0.0546875
- bias_one: float32 [512], P('chan'), may hold values from -3 to 3
- gain_two: float32 [512], replicated, may hold values from 0.1 to 1.9
- shift_two: float32 [512], replicated, may hold values from -3 to 3
- conv_two: bfloat16 [27, 512, 256], P(None, None, 'chan'), may hold values from -0.0546875 to 0.0546875
- cotangent: bfloat16 [256, 128, 512], P('chan', 'tm'), may hold values from -6 to 6
- frame_weight: int32 [128], P('tm'), may hold values from 0 to 4
Outputs:
- grad_features: bfloat16 [512, 64, 128], P('chan', 'tm')
All inputs are finite; a program needn't handle non-finite values.
Results may differ from a plain program's by a relative error of at most 0.0075.
Values may be sent and summed in bfloat16 or wider, within the bound.
A program may use at most 192 MiB of HBM per device.

v0:
```python
import jax
import jax.numpy as jnp
from jax import lax
from jax.sharding import PartitionSpec as P

GROUPS = 32
H1 = 8
W1 = 16


EPS = 1e-06


def from_behind(block, axis, distance):
    devices = range(lax.axis_size(axis))
    route = [(i - distance, i) for i in devices if i - distance in devices]
    return lax.ppermute(block, axis, route)


def spatial_shift(values, height, width, delta_y, delta_x):
    lead = values.shape[:-1]
    grid = values.reshape(lead + (height, width))
    pads = [(0, 0)] * len(lead) + [(1, 1), (1, 1)]
    grid = jnp.pad(grid, pads)
    piece = grid[..., 1 + delta_y : 1 + delta_y + height, 1 + delta_x : 1 + delta_x + width]
    return piece.reshape(lead + (height * width,))


def conv_forward(extended, weight, height, width):
    frames = extended.shape[1] - 2
    moved = [spatial_shift(extended, height, width, tap // 3 - 1, tap % 3 - 1) for tap in range(9)]
    stacked = jnp.stack(
        [moved[tap][:, depth : depth + frames] for depth in range(3) for tap in range(9)], axis=0
    )
    return jnp.einsum("kcts,kco->ots", stacked, weight, preferred_element_type=jnp.float32)


def conv_transpose(extended, weight, height, width):
    frames = extended.shape[1] - 2
    moved = [spatial_shift(extended, height, width, 1 - tap // 3, 1 - tap % 3) for tap in range(9)]
    stacked = jnp.stack(
        [moved[tap][:, 2 - depth : 2 - depth + frames] for depth in range(3) for tap in range(9)],
        axis=0,
    )
    return jnp.einsum("kots,kco->cts", stacked, weight, preferred_element_type=jnp.float32)


def fold_blocks(values):
    rows = values.shape[0]
    frames = values.shape[1] // 2
    blocks = values.reshape(rows, frames, 2, H1, 2, W1, 2)
    return jnp.sum(blocks, axis=(2, 4, 6)).reshape(rows, frames, H1 * W1)


def tm_total(values):
    return lax.psum((values[0], values[1]), "tm")


def group_norm(values, groups):
    grouped = values.reshape(groups, -1)
    count = grouped.shape[1] * lax.axis_size("tm")
    total, squares = tm_total((jnp.sum(grouped, axis=1), jnp.sum(grouped * grouped, axis=1)))
    mean = total / count
    centered = grouped - mean[:, None]
    variance = squares / count - mean * mean
    inverse = lax.rsqrt(variance + EPS)
    return ((centered * inverse[:, None]).reshape(values.shape), inverse)


def group_sums(grad_norm, normed, groups):
    grads = grad_norm.reshape(groups, -1)
    norms = normed.reshape(groups, -1)
    return tm_total((jnp.sum(grads, axis=1), jnp.sum(grads * norms, axis=1)))


def silu_slope(pre):
    sig = jax.nn.sigmoid(pre)
    return sig * (1.0 + pre * (1.0 - sig))


def next_frames(values):
    return from_behind(values, "tm", -1)


def body(
    features,
    gain_one,
    shift_one,
    conv_one,
    bias_one,
    gain_two,
    shift_two,
    conv_two,
    cotangent,
    frame_weight,
):
    half_in, frames, cells = features.shape
    channels = gain_one.shape[0]
    per_group = channels // GROUPS
    my_groups = half_in // per_group
    offset = lax.axis_index("chan") * half_in
    whole = lax.all_gather(features, "chan", axis=0, tiled=True)
    norm1, inv1 = group_norm(whole.astype(jnp.float32), GROUPS)
    pre1 = norm1 * gain_one[:, None, None] + shift_one[:, None, None]
    act1 = jax.nn.silu(pre1).astype(jnp.bfloat16)
    before = from_behind(act1[:, frames - 2 :], "tm", 1)
    hidden = conv_forward(jnp.concatenate([before, act1], axis=1), conv_one, H1, W1)
    hidden = (hidden + bias_one[:, None, None]).astype(jnp.bfloat16)
    gain_mine = lax.dynamic_slice_in_dim(gain_two, offset, half_in, 0)
    shift_mine = lax.dynamic_slice_in_dim(shift_two, offset, half_in, 0)
    norm2, inv2 = group_norm(hidden.astype(jnp.float32), my_groups)
    pre2 = norm2 * gain_mine[:, None, None] + shift_mine[:, None, None]
    slope2 = silu_slope(pre2) * gain_mine[:, None, None]
    scale = frame_weight.astype(jnp.float32) / 4.0
    weighted = (cotangent.astype(jnp.float32) * scale[None, :, None]).astype(jnp.bfloat16)
    cot_ext = jnp.concatenate([weighted, next_frames(weighted[:, :2])], axis=1)
    piece = conv_two
    block_sum = fold_blocks(
        lax.psum_scatter(
            conv_transpose(cot_ext, piece, 2 * H1, 2 * W1), "chan", scatter_dimension=0, tiled=True
        )
    )
    grad_low = block_sum * slope2
    total_one, total_two = group_sums(grad_low, norm2, my_groups)
    count_hi = 8 * per_group * frames * cells * lax.axis_size("tm")
    first = 8.0 * total_one / count_hi
    second = 8.0 * total_two / count_hi
    grouped = (
        grad_low.reshape(my_groups, -1)
        - first[:, None]
        - norm2.reshape(my_groups, -1) * second[:, None]
    )
    grad_hidden = (grouped * inv2[:, None]).reshape(half_in, frames, cells).astype(jnp.bfloat16)
    hid_ext = jnp.concatenate([grad_hidden, next_frames(grad_hidden[:, :2])], axis=1)
    piece = conv_one
    grad_act1 = lax.psum_scatter(
        conv_transpose(hid_ext, piece, H1, W1), "chan", scatter_dimension=0, tiled=True
    )
    norm_mine = lax.dynamic_slice_in_dim(norm1, offset, half_in, 0)
    pre_mine = lax.dynamic_slice_in_dim(pre1, offset, half_in, 0)
    gain_first = lax.dynamic_slice_in_dim(gain_one, offset, half_in, 0)
    inv_mine = lax.dynamic_slice_in_dim(inv1, offset // per_group, my_groups, 0)
    grad_norm1 = grad_act1 * silu_slope(pre_mine) * gain_first[:, None, None]
    sum_one, sum_two = group_sums(grad_norm1, norm_mine, my_groups)
    count_lo = per_group * frames * cells * lax.axis_size("tm")
    result = (
        grad_norm1.reshape(my_groups, -1)
        - (sum_one / count_lo)[:, None]
        - norm_mine.reshape(my_groups, -1) * (sum_two / count_lo)[:, None]
    )
    return (result * inv_mine[:, None]).reshape(half_in, frames, cells).astype(jnp.bfloat16)


def solution(mesh):
    placed = (
        P("chan", "tm", None),
        P(),
        P(),
        P(None, None, "chan"),
        P("chan"),
        P(),
        P(),
        P(None, None, "chan"),
        P("chan", "tm", None),
        P("tm"),
    )
    return jax.shard_map(
        body, mesh=mesh, in_specs=placed, out_specs=P("chan", "tm", None), check_vma=False
    )
```

profile of v0, /device:TPU:0, one launch (start us, length us, event | category | flops | bytes accessed | tf_op | source)
XLA Modules:
  0.0 301.4 jit_solution(15454722771888768950)
XLA Ops:
  6.5 2.8 copy.91
  9.3 0.7 convert_multiply_fusion.1
  10.0 1.5 multiply_convert_fusion
  11.5 1.3 collective-permute-start
  12.8 2.1 collective-permute-done
  15.1 3.8 %pad_slice_fusion.8 = (bf16[128,10,16,32]{0,3,2,1:T(8,128)(2,1)S(1)}, bf16[128,10,16,32]{0,3,2,1:T(8,128)(2,1)S(1)}, bf16[128,10,16,32]{0,3,2,1:T(8,128)(2,1)S(1...) fusion(bf16[128,10,16,32]{0,3,2,1:T(8,128)(2,1)S(1)} %bitcast.532), kind=kLoop, calls=%fused_computation.15 | loop fusion | bytes 11796480 | tf_op jit(solution)/shard_map/slice | solution.py:25
  18.9 1.2 fusion.55
  20.1 1.2 fusion.54
  21.3 1.2 fusion.53
  22.4 1.2 fusion.52
  23.6 1.2 fusion.26
  24.8 1.2 fusion.51
  25.9 1.2 fusion.50
  27.1 1.2 fusion.49
  28.3 1.1 fusion.48
  29.5 1.2 fusion.47
  30.7 1.2 fusion.46
  31.9 1.1 fusion.45
  33.0 1.2 fusion.44
  34.2 1.2 fusion.29
  35.3 1.2 fusion.43
  36.6 1.2 fusion.42
  37.7 1.2 fusion.41
  38.9 1.1 fusion.40
  40.0 1.2 fusion.39
  41.2 1.2 fusion.38
  42.4 1.2 fusion.37
  43.6 1.2 fusion.36
  44.8 1.3 bitcast_dynamic-update-slice_fusion
  46.1 1.2 fusion.35
  47.2 1.2 fusion.34
  48.5 1.2 fusion.33
  49.6 1.2 fusion.32
  50.8 21.6 %fusion.6 = f32[512,8,512]{0,2,1:T(8,128)} fusion(bf16[27,128,8,512]{1,3,0,2:T(8,128)(2,1)} %fusion.32, bf16[27,512,128]{2,1,0:T(8,128)(2,1)S(1)} %copy-done), kind=kOutput, calls=%fused_computation.6 | convolution fusion | flops 14495514624 | bytes 40239104 | tf_op jit(solution)/shard_map/kots,kco->cts/dot_general | solution.py:45
  72.5 0.9 copy-done.3
  73.5 8.0 %all_gather.3 = bf16[512,4,128]{0,2,1:T(8,128)(2,1)S(1)} all-gather(bf16[256,4,128]{0,2,1:T(8,128)(2,1)S(1)} %copy.110), channel_id=1, replica_groups=mesh['tm'=16,'chan'=2] {'chan'}, dimensions={0}, use_global_device_ids=true | all-gather | bytes 786432 | tf_op jit(solution)/shard_map/all_gather | solution.py:102
  82.1 37.3 %all-reduce.6 = (f32[32]{0:T(128)S(1)}, f32[32]{0:T(128)S(1)}) all-reduce(f32[32]{0:T(128)S(1)} %reduce_sum.112, f32[32]{0:T(128)S(1)} %reduce_sum.106), channel_id=1, replica_groups=mesh['tm'=16,'chan'=2] {'tm'}, use_global_device_ids=true, to_apply=%region_7.8 | all-reduce | flops 64 | bytes 512 | tf_op jit(solution)/shard_map/psum | solution.py:56
  119.7 1.8 multiply_add_fusion
  121.5 1.3 collective-permute-start.1
  122.9 1.0 collective-permute-done.1
  124.0 1.8 pad_slice_fusion
  127.1 1.8 slice-done
  128.9 1.0 slice-done.1
  129.9 3.8 %fusion.123 = (f32[256]{0:T(256)S(1)}, f32[256]{0:T(256)S(1)}, f32[4,128,256]{2,1,0:T(8,128)S(1)}) fusion(f32[256]{0:T(256)S(1)} %copy-done.8, bf16[27,512,4,128]{1,3,0,2:T(8,128)(2,1)S(1)} %fusion.62, bf16[27,512,256]{2,1,0:T(8,128)(2,1)S(1)} %bitcast.560), kind=kOutput, calls=%fused_computation.249 | convolution fusion | flops 3624664576 | bytes 21761024 | tf_op jit(solution)/shard_map/kcts,kco->ots/dot_general | solution.py:35
  134.2 29.7 %all-reduce.5 = (f32[16]{0:T(128)S(1)}, f32[16]{0:T(128)S(1)}) all-reduce(f32[16]{0:T(128)S(1)} %reduce_sum.121, f32[16]{0:T(128)S(1)} %reduce_sum.118), channel_id=1, replica_groups=mesh['tm'=16,'chan'=2] {'tm'}, use_global_device_ids=true, to_apply=%region_13.14 | all-reduce | flops 32 | bytes 256 | tf_op jit(solution)/shard_map/psum | solution.py:56
  164.2 13.9 %reduce-scatter.3.cloned.1.call-done = f32[256,8,512]{0,2,1:T(8,128)} async-done(((f32[512,8,512]{0,2,1:T(8,128)}), f32[256,8,512]{0,2,1:T(8,128)}) %reduce-scatter.3.cloned.1.call-update) | async-done | bytes 4194320 | tf_op jit(solution)/shard_map/reduce_scatter | solution.py:119
  178.2 5.8 %reshape.176 = f32[256,4,2,8,2,16,2]{0,6,5,4,3,2,1:T(2,128)} reshape(f32[256,8,512]{0,2,1:T(8,128)} %reduce-scatter.3.cloned.1.call-done) | data formatting | bytes 8388608 | tf_op jit(solution)/shard_map/reshape | solution.py:51
  184.0 4.8 %reduce_sum.103 = f32[256,4,8,16]{0,3,2,1:T(8,128)S(1)} reduce(f32[256,4,2,8,2,16,2]{0,6,5,4,3,2,1:T(2,128)} %reshape.176, f32[]{:T(128)} %constant.43.clone.1), dimensions={2,4,6}, to_apply=%region_1.0 | reduce | flops 917504 | bytes 4718596 | tf_op jit(solution)/shard_map/reduce_sum | solution.py:52
  189.5 33.2 %all-reduce.4 = (f32[16]{0:T(128)S(1)}, f32[16]{0:T(128)S(1)}) all-reduce(f32[16]{0:T(128)S(1)} %reduce_sum.155, f32[16]{0:T(128)S(1)} %reduce_sum.152), channel_id=1, replica_groups=mesh['tm'=16,'chan'=2] {'tm'}, use_global_device_ids=true, to_apply=%region_19.20 | all-reduce | flops 32 | bytes 256 | tf_op jit(solution)/shard_map/psum | solution.py:56
  223.1 1.5 collective-permute-start.2
  224.7 1.7 collective-permute-done.2
  227.6 1.0 slice-done.2
  228.6 1.1 slice-done.3
  229.7 4.8 %fusion.9 = f32[512,4,128]{0,2,1:T(8,128)} fusion(bf16[27,256,4,128]{1,3,2,0:T(8,128)(2,1)S(1)} %fusion.97, bf16[27,512,256]{2,1,0:T(8,128)(2,1)S(1)} %bitcast.562), kind=kOutput, calls=%fused_computation.30 | convolution fusion | flops 3623878656 | bytes 15204352 | tf_op jit(solution)/shard_map/kots,kco->cts/dot_general | solution.py:45
  234.6 0.6 dynamic_slice.23
  235.2 16.1 %reduce-scatter.5.cloned.1.call-done = f32[256,4,128]{0,2,1:T(8,128)} async-done(((f32[512,4,128]{0,2,1:T(8,128)}), f32[256,4,128]{0,2,1:T(8,128)}) %reduce-scatter.5.cloned.1.call-update) | async-done | bytes 524304 | tf_op jit(solution)/shard_map/reduce_scatter | solution.py:136
  251.3 2.4 fusion.121
  254.0 0.7 reduce_sum.161
  254.7 0.7 mul.202
  255.5 33.7 %all-reduce.3 = (f32[16]{0:T(128)S(1)}, f32[16]{0:T(128)}) all-reduce(f32[16]{0:T(128)} %reduce_sum.161, f32[16]{0:T(128)S(1)} %reduce_sum.158), channel_id=1, replica_groups=mesh['tm'=16,'chan'=2] {'tm'}, use_global_device_ids=true, to_apply=%region_26.27 | all-reduce | flops 32 | bytes 256 | tf_op jit(solution)/shard_map/psum | solution.py:56
  289.3 0.7 broadcast_multiply_fusion.1
  290.1 0.6 sub.100
  290.7 2.0 multiply_convert_fusion.2
  292.7 1.8 copy.129
  (130 shorter events, 6.1 us)
Async XLA Ops:
  6.5 44.3 %copy-start = (bf16[27,512,128]{2,1,0:T(8,128)(2,1)S(1)}, bf16[27,512,128]{2,1,0:T(8,128)(2,1)}, u32[]{:S(2)}) copy-start(bf16[27,512,128]{2,1,0:T(8,128)(2,1)} %param.17) | copy-start | bytes 10616836
  6.5 171.6 %reduce-scatter.3.cloned.1.call-start = ((), (), s32[]{:S(2)}) async-start(), calls=%async_computation.2 | async-start | bytes 12582912 | tf_op jit(solution)/shard_map/reduce_scatter | solution.py:119
  11.5 3.4 %collective-permute-start = (bf16[128,2,512]{0,2,1:T(8,128)(2,1)S(1)}, bf16[128,2,512]{0,2,1:T(8,128)(2,1)S(1)}, u32[]{:S(2)}, u32[]{:S(2)}) collective-permute-start(bf16[128,2,512]{0,2,1:T(8,128)(2,1)S(1)} %slice.426), channel_id=1, source_target_pairs={{2,0},{4,2},{6,4},{8,6},{10,8},{12,10},{14,12},{16,14},{18,16},{20... | collective-permute-start | bytes 786440 | tf_op jit(solution)/shard_map/ppermute | solution.py:17
  36.5 8.2 %copy-start.2 = (bf16[128,8,512]{0,2,1:T(8,128)(2,1)S(1)}, bf16[128,8,512]{0,2,1:T(8,128)(2,1)}, u32[]{:S(2)}) copy-start(bf16[128,8,512]{0,2,1:T(8,128)(2,1)} %copy.91) | copy-start | bytes 3145732
  72.4 0.9 copy-start.3
  72.4 47.3 %copy-start.4 = (f32[512]{0:T(512)S(1)}, f32[512]{0:T(512)}, u32[]{:S(2)}) copy-start(f32[512]{0:T(512)} %param.11) | copy-start | bytes 6148
  72.4 47.3 %copy-start.5 = (f32[512]{0:T(512)S(1)}, f32[512]{0:T(512)}, u32[]{:S(2)}) copy-start(f32[512]{0:T(512)} %param.12) | copy-start | bytes 6148
  72.4 50.4 %copy-start.6 = (f32[512]{0:T(512)S(1)}, f32[512]{0:T(512)}, u32[]{:S(2)}) copy-start(f32[512]{0:T(512)} %param.15) | copy-start | bytes 6148
  72.4 178.9 %reduce-scatter.5.cloned.1.call-start = ((), (), s32[]{:S(2)}) async-start(), calls=%async_computation.3 | async-start | bytes 1572864 | tf_op jit(solution)/shard_map/reduce_scatter | solution.py:136
  121.5 2.4 collective-permute-start.1
  126.4 2.4 slice-start
  126.5 2.4 copy-start.8
  126.7 3.2 %slice-start.1 = ((s8[7077888]{0:T(1024)(128)(4,1)}), s8[2883584]{0:T(1024)(128)(4,1)S(1)}, s32[]{:S(2)}) async-start(s8[7077888]{0:T(1024)(128)(4,1)} %bitcast.559), calls=%async_computation.5 | async-start | bytes 5767168
  129.9 4.2 %copy-start.7 = (f32[512]{0:T(512)S(1)}, f32[512]{0:T(512)}, u32[]{:S(2)}) copy-start(f32[512]{0:T(512)} %param.16) | copy-start | bytes 6148
  223.1 3.2 %collective-permute-start.2 = (bf16[256,2,128]{0,2,1:T(8,128)(2,1)S(1)}, bf16[256,2,128]{0,2,1:T(8,128)(2,1)S(1)}, u32[]{:S(2)}, u32[]{:S(2)}) collective-permute-start(bf16[256,2,128]{0,2,1:T(8,128)(2,1)S(1)} %slice.484), channel_id=1, source_target_pairs={{2,0},{4,2},{6,4},{8,6},{10,8},{12,10},{14,12},{16,14},{18,16},{20... | collective-permute-start | bytes 393224 | tf_op jit(solution)/shard_map/ppermute | solution.py:17
  226.4 2.2 slice-start.2
  227.2 2.6 slice-start.3
  229.7 64.8 %copy-start.1 = (bf16[27,512,128]{2,1,0:T(8,128)(2,1)S(1)}, bf16[27,512,128]{2,1,0:T(8,128)(2,1)}, u32[]{:S(2)}) copy-start(bf16[27,512,128]{2,1,0:T(8,128)(2,1)} %param.17) | copy-start | bytes 10616836
Sparse Core Ops, SparseCore 0:
  72.6 105.5 reduce-scatter.2
  234.7 16.6 reduce-scatter.4
where the time goes:
time: 302 us; the launch traced here: 301 us
  blocking collectives  142 us (47%)
  local copies, waits for them, and re-layouts  56.2 us (19%)
  waiting for transfers between devices  35 us (12%)
  matrix products  30.3 us (10%)
  other arithmetic  20 us (7%)
  between operations  14.1 us (5%)
  starting transfers between devices  4.15 us (1%)
    psum x4, blocking collectives, tm_total(): return lax.psum((values[0], values[1]), 'tm')  134 us
    unnamed x99, local copies, waits for them, and re-layouts  37.2 us
    dot_general x2, matrix products, conv_transpose(): jnp.einsum('kots,kco->cts', stacked, weight, preferred_element_type=jnp.f...  26.4 us
    reduce_scatter x1, waiting for transfers between devices, body(): lax.psum_scatter(conv_transpose(hid_ext, piece, H1, W1), 'chan', scatter_...  16.1 us
    reduce_scatter x1, waiting for transfers between devices, body(): lax.psum_scatter(conv_transpose(cot_ext, piece, 2 * H1, 2 * W1), 'chan',...  13.9 us
    all_gather x1, blocking collectives, body(): whole = lax.all_gather(features, 'chan', axis=0, tiled=True)  7.98 us
  transfers between devices with their start and end apart: 5, of which 5 were waited for; matrix products, arithmetic and copies ran while one was open for 4% of the time, Pallas kernels for 0%

commit v1 on v0

--- a/solution.py
+++ b/solution.py
@@ -1,6 +1,10 @@
+import functools
+
 import jax
 import jax.numpy as jnp
 from jax import lax
+from jax.experimental import pallas as pl
+from jax.experimental.pallas import tpu as pltpu
 from jax.sharding import PartitionSpec as P
 
 GROUPS = 32
@@ -45,15 +49,90 @@
     return jnp.einsum("kots,kco->cts", stacked, weight, preferred_element_type=jnp.float32)
 
 
-def fold_blocks(values):
-    rows = values.shape[0]
-    frames = values.shape[1] // 2
-    blocks = values.reshape(rows, frames, 2, H1, 2, W1, 2)
-    return jnp.sum(blocks, axis=(2, 4, 6)).reshape(rows, frames, H1 * W1)
+def total_kernel(n, x_ref, o_ref, slots, send_sem, recv_sem):
+    me = lax.axis_index("tm")
+    barrier = pltpu.get_barrier_semaphore()
+    for k in range(1, n):
+        pl.semaphore_signal(
+            barrier, inc=1, device_id={"tm": lax.rem(me + k, n)}, device_id_type=pl.DeviceIdType.MESH
+        )
+    pl.semaphore_wait(barrier, n - 1)
+    copies = []
+    for k in range(1, n):
+        copy = pltpu.make_async_remote_copy(
+            src_ref=x_ref,
+            dst_ref=slots.at[k],
+            send_sem=send_sem.at[k],
+            recv_sem=recv_sem.at[k],
+            device_id={"tm": lax.rem(me + k, n)},
+            device_id_type=pl.DeviceIdType.MESH,
+        )
+        copy.start()
+        copies.append(copy)
+    for copy in copies:
+        copy.wait()
+    total = x_ref[...]
+    for k in range(1, n):
+        total = total + slots[k]
+    o_ref[...] = total
 
 
 def tm_total(values):
-    return lax.psum((values[0], values[1]), "tm")
+    n = lax.axis_size("tm")
+    groups = values[0].shape[0]
+    tile = jnp.pad(jnp.stack(values), ((0, 6), (0, 128 - groups)))
+    out = pl.pallas_call(
+        functools.partial(total_kernel, n),
+        out_shape=jax.ShapeDtypeStruct((8, 128), jnp.float32),
+        in_specs=[pl.BlockSpec(memory_space=pltpu.VMEM)],
+        out_specs=pl.BlockSpec(memory_space=pltpu.VMEM),
+        scratch_shapes=[
+            pltpu.VMEM((n, 8, 128), jnp.float32),
+            pltpu.SemaphoreType.DMA((n,)),
+            pltpu.SemaphoreType.DMA((n,)),
+        ],
+        compiler_params=pltpu.CompilerParams(collective_id=0, has_side_effects=True),
+    )(tile)
+    return out[0, :groups], out[1, :groups]
+
+
+def pooling(height, width):
+    fine = lax.broadcasted_iota(jnp.int32, (4 * height * width, 9, height * width), 0)
+    tap = lax.broadcasted_iota(jnp.int32, fine.shape, 1)
+    cell = lax.broadcasted_iota(jnp.int32, fine.shape, 2)
+    down = fine // (2 * width) - (2 * (cell // width) + 1 - tap // 3)
+    across = fine % (2 * width) - (2 * (cell % width) + 1 - tap % 3)
+    hit = (down >= 0) & (down <= 1) & (across >= 0) & (across <= 1)
+    return hit.astype(jnp.bfloat16).reshape(fine.shape[0], -1)
+
+
+def conv_transpose_folded(weighted, weight):
+    rows, frames, cells = weighted.shape
+    low = frames // 2
+    pooled = jnp.einsum(
+        "ots,sq->otq", weighted, pooling(H1, W1), preferred_element_type=jnp.float32
+    ).reshape(rows, low, 2, 9, cells // 4)
+    even = pooled[:, :, 0] + pooled[:, :, 1]
+    after = next_frames(even[:, :1].astype(jnp.bfloat16))
+    first = next_frames(pooled[:, :1, 0].astype(jnp.bfloat16)).astype(jnp.float32)
+    odd = pooled[:, :, 1] + jnp.concatenate([pooled[:, 1:, 0], first], axis=1)
+    even = even.astype(jnp.bfloat16)
+    odd = odd.astype(jnp.bfloat16)
+    stacked = jnp.stack([jnp.concatenate([even[:, 1:], after], axis=1), odd, even], axis=0)
+    return jnp.einsum(
+        "dotks,dkco->cts",
+        stacked,
+        weight.reshape(3, 9, weight.shape[1], rows),
+        preferred_element_type=jnp.float32,
+    )
+
+
+def chan_scatter(partial, half):
+    me = lax.axis_index("chan")
+    mine = lax.dynamic_slice_in_dim(partial, me * half, half, 0)
+    other = lax.dynamic_slice_in_dim(partial, (1 - me) * half, half, 0)
+    got = lax.ppermute(other.astype(jnp.bfloat16), "chan", [(0, 1), (1, 0)])
+    return mine + got.astype(jnp.float32)
 
 
 def group_norm(values, groups):
@@ -113,13 +192,7 @@
     slope2 = silu_slope(pre2) * gain_mine[:, None, None]
     scale = frame_weight.astype(jnp.float32) / 4.0
     weighted = (cotangent.astype(jnp.float32) * scale[None, :, None]).astype(jnp.bfloat16)
-    cot_ext = jnp.concatenate([weighted, next_frames(weighted[:, :2])], axis=1)
-    piece = conv_two
-    block_sum = fold_blocks(
-        lax.psum_scatter(
-            conv_transpose(cot_ext, piece, 2 * H1, 2 * W1), "chan", scatter_dimension=0, tiled=True
-        )
-    )
+    block_sum = chan_scatter(conv_transpose_folded(weighted, conv_two), half_in)
     grad_low = block_sum * slope2
     total_one, total_two = group_sums(grad_low, norm2, my_groups)
     count_hi = 8 * per_group * frames * cells * lax.axis_size("tm")
@@ -132,10 +205,7 @@
     )
     grad_hidden = (grouped * inv2[:, None]).reshape(half_in, frames, cells).astype(jnp.bfloat16)
     hid_ext = jnp.concatenate([grad_hidden, next_frames(grad_hidden[:, :2])], axis=1)
-    piece = conv_one
-    grad_act1 = lax.psum_scatter(
-        conv_transpose(hid_ext, piece, H1, W1), "chan", scatter_dimension=0, tiled=True
-    )
+    grad_act1 = chan_scatter(conv_transpose(hid_ext, conv_one, H1, W1), half_in)
     norm_mine = lax.dynamic_slice_in_dim(norm1, offset, half_in, 0)
     pre_mine = lax.dynamic_slice_in_dim(pre1, offset, half_in, 0)
     gain_first = lax.dynamic_slice_in_dim(gain_one, offset, half_in, 0)

time: 302 us -> 158 us (0.52)
  blocking collectives: 142 us -> 10.2 us
  Pallas kernels: 0 us -> 40.9 us
  waiting for transfers between devices: 35 us -> 11.3 us
  local copies, waits for them, and re-layouts: 56.2 us -> 33.6 us
  matrix products: 30.3 us -> 12.5 us
  other arithmetic: 20 us -> 37.1 us
  between operations: 14.1 us -> 0.78 us
  starting transfers between devices: 4.15 us -> 10 us
    psum x4 -> x0, blocking collectives: 134 us -> none  [tm_total(): return lax.psum((values[0], values[1]), 'tm')]
    pallas_call x0 -> x4, Pallas kernels: none -> 40.9 us  [tm_total(): pl.pallas_call(functools.partial(total_kernel, n), out_shape=jax.ShapeDty...]
    reduce_scatter x2 -> x0, waiting for transfers between devices: 30 us -> none  [the longest x1 16.1 us: body(): lax.psum_scatter(conv_transpose(hid_ext, piece, H1, W1), 'chan', scatter_...]
    unnamed x99 -> x85, local copies, waits for them, and re-layouts: 37.2 us -> 10 us
    dot_general x2 -> x1, matrix products: 26.4 us -> 3.84 us  [conv_transpose(): jnp.einsum('kots,kco->cts', stacked, weight, preferred_element_type=jnp.f...]
    ppermute x0 -> x2, waiting for transfers between devices: none -> 9.58 us  [chan_scatter(): got = lax.ppermute(other.astype(jnp.bfloat16), 'chan', [(0, 1), (1, 0)])]
    convert_element_type x0 -> x3, other arithmetic: none -> 6.91 us  [the longest x1 3.7 us: conv_transpose_folded(): odd = odd.astype(jnp.bfloat16)]
    reshape x1 -> x0, local copies, waits for them, and re-layouts: 5.82 us -> none  [fold_blocks(): blocks = values.reshape(rows, frames, 2, H1, 2, W1, 2)]
  transfers between devices with their start and end apart: 5 -> 6, of which waited for: 5 -> 3; matrix products, arithmetic and copies ran while one was open for 4% -> 20% of each run, Pallas kernels for 0% -> 7%
where the time goes in v1:
time: 158 us; the launch traced here: 156 us
  Pallas kernels  40.9 us (26%)
  other arithmetic  37.1 us (23%)
  local copies, waits for them, and re-layouts  33.6 us (21%)
  matrix products  12.5 us (8%)
  waiting for transfers between devices  11.3 us (7%)
  blocking collectives  10.2 us (6%)
  starting transfers between devices  10 us (6%)
    pallas_call x4, Pallas kernels, tm_total(): pl.pallas_call(functools.partial(total_kernel, n), out_shape=jax.ShapeDty...  40.9 us
    all_gather x1, blocking collectives, body(): whole = lax.all_gather(features, 'chan', axis=0, tiled=True)  10.2 us
    unnamed x85, local copies, waits for them, and re-layouts  10 us
    ppermute x2, waiting for transfers between devices, chan_scatter(): got = lax.ppermute(other.astype(jnp.bfloat16), 'chan', [(0, 1), (1, 0)])  9.58 us
    reduce_sum x6, other arithmetic, group_sums(): return tm_total((jnp.sum(grads, axis=1), jnp.sum(grads * norms, axis=1)))  7.21 us
    ppermute x4, starting transfers between devices, from_behind(): return lax.ppermute(block, axis, route)  6.97 us
    dot_general x1, matrix products, conv_forward(): jnp.einsum('kcts,kco->ots', stacked, weight, preferred_element_type=jnp.f...  4.61 us
    dot_general x1, matrix products, conv_transpose(): jnp.einsum('kots,kco->cts', stacked, weight, preferred_element_type=jnp.f...  3.84 us
  transfers between devices with their start and end apart: 6, of which 3 were waited for; matrix products, arithmetic and copies ran while one was open for 20% of the time, Pallas kernels for 7%

profile of v1, /device:TPU:0, one launch (start us, length us, event | category | flops | bytes accessed | tf_op | source)
XLA Modules:
  0.0 156.4 jit_solution(16803919286198200214)
XLA Ops:
  0.0 2.0 %copy.31 = bf16[256,4,128]{0,2,1:T(8,128)(2,1)} copy(bf16[256,4,128]{2,1,0:T(4,128)(2,1)} %param.10) | data formatting | bytes 524288 | tf_op args[0]
  2.0 10.2 %all_gather.3 = bf16[512,4,128]{0,2,1:T(8,128)(2,1)S(1)} all-gather(bf16[256,4,128]{0,2,1:T(8,128)(2,1)} %copy.31), channel_id=1, replica_groups=mesh['tm'=16,'chan'=2] {'chan'}, dimensions={0}, use_global_device_ids=true | all-gather | bytes 786432 | tf_op jit(solution)/shard_map/all_gather | solution.py:181
  12.2 0.8 copy-done.4
  12.9 0.8 convert_reduce_fusion
  13.7 0.8 reduce_sum.96
  14.5 1.4 reduce_sum.99
  15.8 0.7 reduce_sum.97
  16.5 0.8 reduce_sum.100
  17.4 1.3 select_maximum_fusion.3.x_ref
  18.7 8.9 %shard_map.100 = f32[8,128]{1,0:T(8,128)} custom-call(f32[8,128]{1,0:T(8,128)} %select_maximum_fusion.3.x_ref), custom_call_target="tpu_custom_call" | custom-call | tf_op jit(solution)/shard_map/pallas_call | solution.py:84
  27.5 0.8 fusion.147
  28.3 1.2 multiply_bitcast_fusion.5
  31.6 2.8 %multiply_convert_fusion.1 = (bf16[512,4,128]{0,2,1:T(8,128)(2,1)S(1)}, f32[512,4,128]{0,2,1:T(8,128)}, f32[512,4,128]{0,2,1:T(8,128)}) fusion(f32[512]{0:T(512)} %param.12, f32[512]{0:T(512)} %param.11, f32[512]{0:T(512)} %mul.207, f32[512]{0:T(512)} %sub.162, bf16[512,4,128]{0,2,1:T(8,128)(2,1)} %copy-done.4), kind=kLoop, calls=%fused_computation.82 | loop fusion | flops 2621440 | bytes 3153920 | tf_op jit(solution)/shard_map/convert_element_type | solution.py:184
  34.4 0.8 slice.349
  35.2 2.7 %collective-permute-start.3 = (bf16[512,2,128]{0,2,1:T(8,128)(2,1)}, bf16[512,2,128]{0,2,1:T(8,128)(2,1)}, u32[]{:S(2)}, u32[]{:S(2)}) collective-permute-start(bf16[512,2,128]{0,2,1:T(8,128)(2,1)} %slice.349), channel_id=1, source_target_pairs={{0,2},{2,4},{4,6},{6,8},{8,10},{10,12},{12,14},{14,16},{16,18},{18... | collective-permute-start | bytes 786440 | tf_op jit(solution)/shard_map/ppermute | solution.py:21
  38.6 1.6 %multiply_convert_fusion = bf16[128,8,512]{2,1,0:T(8,128)(2,1)S(1)} fusion(bf16[128,8,512]{2,1,0:T(8,128)(2,1)} %param.18, f32[8]{0:T(128)S(1)} %convert_multiply_fusion.1), kind=kLoop, calls=%fused_computation.35 | loop fusion | flops 1572864 | bytes 2097184 | tf_op jit(solution)/shard_map/convert_element_type | solution.py:194
  40.6 2.0 %fusion.21 = f32[128,4,2,9,128]{4,0,3,2,1:T(8,128)S(1)} fusion(bf16[128,4,2,512,1]{3,0,4,2,1:T(8,128)(2,1)S(1)} %bitcast.432, s32[9]{0:T(128)S(1)} %get-tuple-element.52, s32[9]{0:T(128)S(1)} %get-tuple-element.58, s32[128]{0:T(128)S(1)} %get-tuple-element.54, s32[128]{0:T(128)S(1)} %get-tuple-element.55, s32[512]{0:T(512)S(1)} %get-tuple-element.48, ...), kind=kOutput, calls=%fused_computation.34 | convolution fusion | flops 1220345856 | bytes 5778850 | tf_op jit(solution)/shard_map/ots,sq->otq/dot_general | solution.py:112
  42.6 0.8 fusion.103
  43.4 1.3 collective-permute-start.1
  45.2 0.7 slice.346
  45.9 1.5 collective-permute-start
  47.4 1.1 slice.345
  49.8 2.9 %slice_bitcast_fusion = f32[1,128,3,9,128]{4,1,3,2,0:T(8,128)} fusion(f32[128,4,2,9,128]{4,0,3,2,1:T(8,128)} %copy-done.1), kind=kLoop, calls=%fused_computation.36 | loop fusion | bytes 3538944 | tf_op jit(solution)/shard_map/concatenate | solution.py:118
  52.7 1.2 pad_maximum_fusion
  53.9 1.8 %pad_slice_fusion = (bf16[512,6,8,16]{0,3,2,1:T(8,128)(2,1)S(1)}, bf16[512,6,8,16]{0,3,2,1:T(8,128)(2,1)S(1)}, bf16[512,6,8,16]{0,3,2,1:T(8,128)(2,1)S(1)}, bf16...) fusion(bf16[512,6,8,16]{0,3,2,1:T(8,128)(2,1)S(1)} %bitcast.430), kind=kLoop, calls=%fused_computation.10 | loop fusion | bytes 7077888 | tf_op jit(solution)/shard_map/slice | solution.py:29
  55.9 1.0 fusion.67
  57.3 1.1 fusion.70
  59.5 1.1 slice-done.1
  60.6 4.6 %fusion.153 = (f32[256]{0:T(256)S(1)}, f32[256]{0:T(256)S(1)}, f32[4,128,256]{2,1,0:T(8,128)}) fusion(f32[256]{0:T(256)S(1)} %copy-done.13, bf16[27,512,4,128]{1,3,2,0:T(8,128)(2,1)S(1)} %fusion.71, bf16[27,512,256]{2,1,0:T(8,128)(2,1)S(1)} %bitcast.442), kind=kOutput, calls=%fused_computation.276 | convolution fusion | flops 3624664576 | bytes 21761024 | tf_op jit(solution)/shard_map/kcts,kco->ots/dot_general | solution.py:39
  66.2 11.3 %shard_map.101 = f32[8,128]{1,0:T(8,128)} custom-call(f32[8,128]{1,0:T(8,128)} %select_maximum_fusion.2.x_ref), custom_call_target="tpu_custom_call" | custom-call | tf_op jit(solution)/shard_map/pallas_call | solution.py:84
  77.6 1.1 bitcast_convert_fusion
  78.7 3.7 %fusion.10 = (bf16[1,128,4,9,128]{4,1,3,2,0:T(8,128)(2,1)S(1)}, bf16[1,128,4,9,128]{4,1,3,2,0:T(8,128)(2,1)S(1)}) fusion(f32[1,128,1,9,128]{4,1,3,2,0:T(8,128)S(1)} %bitcast_convert_fusion, f32[1,128,3,9,128]{4,1,3,2,0:T(8,128)} %slice_bitcast_fusion, f32[128,4,2,9,128]{4,0,3,2,1:T(8,128)} %copy-done.1), kind=kLoop, calls=%fused_computation.19 | loop fusion | flops 2949120 | bytes 9437184 | tf_op jit(solution)/shard_map/convert_element_type | solution.py:120
  82.4 1.1 maximum_bitcast_fusion
  83.5 2.1 %fusion.23 = f32[4,128,512]{2,1,0:T(8,128)S(1)} fusion(bf16[3,9,512,128,1]{3,2,1,4,0:T(8,128)(2,1)S(1)} %bitcast.381, bf16[1,128,4,9,128]{4,1,3,2,0:T(8,128)(2,1)S(1)} %get-tuple-element.16, bf16[1,128,4,9,128]{4,1,3,2,0:T(8,128)(2,1)S(1)} %get-tuple-element.15, bf16[1,128,4,9,128]{4,1,3,2,0:T(8,128)(2,1)S(1)} %maximum_bitcast_fusion), kind=kOutput, calls=%fused_computation.40 | convolution fusion | flops 1815478272 | bytes 8126464 | tf_op jit(solution)/shard_map/dotks,dkco->cts/dot_general | solution.py:122
  85.6 1.0 copy-done.6
  86.6 0.7 fusion.110
  87.3 1.5 collective-permute-start.2
  88.9 0.8 fusion.145
  89.8 0.7 multiply_bitcast_fusion.4
  90.6 5.3 %collective-permute-done.2 = bf16[256,4,128]{0,2,1:T(8,128)(2,1)} collective-permute-done((bf16[256,4,128]{0,2,1:T(8,128)(2,1)}, bf16[256,4,128]{0,2,1:T(8,128)(2,1)}, u32[]{:S(2)}, u32[]{:S(2)}) %collective-permute-start.2) | collective-permute-done | bytes 262176 | tf_op jit(solution)/shard_map/ppermute | solution.py:134
  96.0 3.0 %fusion.152 = (f32[256]{0:T(256)}, f32[256]{0:T(256)}, f32[256,4,128]{0,2,1:T(8,128)}) fusion(f32[256]{0:T(256)S(1)} %mul.216, f32[4,128,256]{2,1,0:T(8,128)} %get-tuple-element.40, f32[256]{0:T(256)S(1)} %sub.167, f32[256]{0:T(256)} %dynamic_slice.33, f32[256]{0:T(256)} %dynamic_slice.32, bf16[256,4,128]{0,2,1:T(8,128)(2,1)} %collective-permute-done.2, ...), kind=kLoop, calls=%fused_computation.275 | loop fusion | flops 2358784 | bytes 1841156 | tf_op jit(solution)/shard_map/reduce_sum | solution.py:152
  99.0 0.8 reduce_sum.114
  99.8 0.7 reduce_sum.115
  100.5 0.8 reduce_sum.144
  101.2 0.7 reduce_sum.145
  101.9 1.3 select_maximum_fusion.1.x_ref
  103.2 8.2 %shard_map.102 = f32[8,128]{1,0:T(8,128)} custom-call(f32[8,128]{1,0:T(8,128)} %select_maximum_fusion.1.x_ref), custom_call_target="tpu_custom_call" | custom-call | tf_op jit(solution)/shard_map/pallas_call | solution.py:84
  111.5 1.3 multiply_bitcast_fusion.3
  113.5 0.7 sub.173
  114.8 1.3 fusion.101
  116.2 1.5 collective-permute-start.4
  117.7 1.7 %collective-permute-done.4 = bf16[256,2,128]{0,2,1:T(8,128)(2,1)S(1)} collective-permute-done((bf16[256,2,128]{0,2,1:T(8,128)(2,1)S(1)}, bf16[256,2,128]{0,2,1:T(8,128)(2,1)S(1)}, u32[]{:S(2)}, u32[]{:S(2)}) %collective-permute-start.4) | collective-permute-done | bytes 131104 | tf_op jit(solution)/shard_map/ppermute | solution.py:21
  120.7 1.0 slice-done.2
  121.7 1.1 slice-done.3
  122.8 3.8 %fusion.26 = f32[4,128,512]{2,1,0:T(8,128)S(1)} fusion(bf16[27,256,4,128]{1,3,2,0:T(8,128)(2,1)S(1)} %fusion.112, bf16[27,512,256]{2,1,0:T(8,128)(2,1)S(1)} %bitcast.444), kind=kOutput, calls=%fused_computation.41 | convolution fusion | flops 3623878656 | bytes 15204352 | tf_op jit(solution)/shard_map/kots,kco->cts/dot_general | solution.py:49
  126.6 1.0 copy-done.7
  127.6 0.7 fusion.111
  128.3 1.5 collective-permute-start.5
  131.3 4.2 %collective-permute-done.5 = bf16[256,4,128]{0,2,1:T(8,128)(2,1)} collective-permute-done((bf16[256,4,128]{0,2,1:T(8,128)(2,1)}, bf16[256,4,128]{0,2,1:T(8,128)(2,1)}, u32[]{:S(2)}, u32[]{:S(2)}) %collective-permute-start.5) | collective-permute-done | bytes 262176 | tf_op jit(solution)/shard_map/ppermute | solution.py:134
  135.6 2.5 %fusion.151 = (f32[256]{0:T(256)S(1)}, f32[256]{0:T(256)S(1)}, f32[256,4,128]{0,2,1:T(8,128)}) fusion(f32[512,4,128]{0,2,1:T(8,128)} %get-tuple-element.27, s32[]{:T(128)S(6)} %select_n.94, f32[256]{0:T(256)} %dynamic_slice.37, f32[512,4,128]{0,2,1:T(8,128)} %get-tuple-element.26, bf16[256,4,128]{0,2,1:T(8,128)(2,1)} %collective-permute-done.5, ...), kind=kLoop, calls=%fused_computation.274 | loop fusion | flops 1834496 | bytes 2362372 | tf_op jit(solution)/shard_map/reduce_sum | solution.py:152
  139.1 12.4 %shard_map.103 = f32[8,128]{1,0:T(8,128)} custom-call(f32[8,128]{1,0:T(8,128)} %select_maximum_fusion.x_ref), custom_call_target="tpu_custom_call" | custom-call | tf_op jit(solution)/shard_map/pallas_call | solution.py:84
  151.5 0.8 multiply_bitcast_fusion.1
  152.6 2.0 %multiply_convert_fusion.2 = bf16[256,4,128]{0,2,1:T(8,128)(2,1)} fusion(f32[256,4,128]{0,2,1:T(8,128)} %get-tuple-element.13, f32[512,4,128]{0,2,1:T(8,128)} %get-tuple-element.27, s32[]{:T(128)S(6)} %select_n.94, f32[256]{0:T(256)} %mul.242, f32[256]{0:T(256)S(1)} %mul.238, f32[256]{0:T(256)S(1)} %sub.180), kind=kLoop, calls=%fused_computation.158 | loop fusion | flops 655360 | bytes 1313796 | tf_op jit(solution)/shard_map/convert_element_type | solution.py:221
  154.6 1.8 %copy.32 = bf16[256,4,128]{2,1,0:T(4,128)(2,1)} copy(bf16[256,4,128]{0,2,1:T(8,128)(2,1)} %multiply_convert_fusion.2) | data formatting | bytes 524288 | tf_op jit(solution)/shard_map/convert_element_type | solution.py:221
  (133 shorter events, 13.0 us)
Async XLA Ops:
  0.0 83.5 %copy-start = (bf16[27,512,128]{2,1,0:T(8,128)(2,1)S(1)}, bf16[27,512,128]{2,1,0:T(8,128)(2,1)}, u32[]{:S(2)}) copy-start(bf16[27,512,128]{2,1,0:T(8,128)(2,1)} %param.17) | copy-start | bytes 10616836
  12.2 0.8 copy-start.4
  28.3 1.2 copy-start.9
  34.4 6.2 %copy-start.2 = (bf16[512,4,128]{0,2,1:T(8,128)(2,1)}, bf16[512,4,128]{0,2,1:T(8,128)(2,1)S(1)}, u32[]{:S(2)}) copy-start(bf16[512,4,128]{0,2,1:T(8,128)(2,1)S(1)} %get-tuple-element.25) | copy-start | bytes 1572868
  35.2 17.5 %collective-permute-start.3 = (bf16[512,2,128]{0,2,1:T(8,128)(2,1)}, bf16[512,2,128]{0,2,1:T(8,128)(2,1)}, u32[]{:S(2)}, u32[]{:S(2)}) collective-permute-start(bf16[512,2,128]{0,2,1:T(8,128)(2,1)} %slice.349), channel_id=1, source_target_pairs={{0,2},{2,4},{4,6},{6,8},{8,10},{10,12},{12,14},{14,16},{16,18},{18... | collective-permute-start | bytes 786440 | tf_op jit(solution)/shard_map/ppermute | solution.py:21
  42.6 2.2 %copy-start.1 = (f32[128,4,2,9,128]{4,0,3,2,1:T(8,128)}, f32[128,4,2,9,128]{4,0,3,2,1:T(8,128)S(1)}, u32[]{:S(2)}) copy-start(f32[128,4,2,9,128]{4,0,3,2,1:T(8,128)S(1)} %fusion.21) | copy-start | bytes 14155780
  42.6 5.9 %copy-start.11 = (f32[512]{0:T(512)S(1)}, f32[512]{0:T(512)}, u32[]{:S(2)}) copy-start(f32[512]{0:T(512)} %param.15) | copy-start | bytes 6148
  42.6 6.5 %copy-start.12 = (f32[512]{0:T(512)S(1)}, f32[512]{0:T(512)}, u32[]{:S(2)}) copy-start(f32[512]{0:T(512)} %param.16) | copy-start | bytes 6148
  43.4 34.2 %collective-permute-start.1 = (bf16[128,1,9,128]{3,0,2,1:T(8,128)(2,1)}, bf16[128,1,9,128]{3,0,2,1:T(8,128)(2,1)}, u32[]{:S(2)}, u32[]{:S(2)}) collective-permute-start(bf16[128,1,9,128]{3,0,2,1:T(8,128)(2,1)} %fusion.103), channel_id=1, source_target_pairs={{2,0},{4,2},{6,4},{8,6},{10,8},{12,10},{14,12},{16,14},{18,16},{20... | collective-permute-start | bytes 884744 | tf_op jit(solution)/shard_map/ppermute | solution.py:21
  45.9 36.5 %collective-permute-start = (bf16[128,1,9,128]{3,0,2,1:T(8,128)(2,1)}, bf16[128,1,9,128]{3,0,2,1:T(8,128)(2,1)}, u32[]{:S(2)}, u32[]{:S(2)}) collective-permute-start(bf16[128,1,9,128]{3,0,2,1:T(8,128)(2,1)} %slice.346), channel_id=1, source_target_pairs={{2,0},{4,2},{6,4},{8,6},{10,8},{12,10},{14,12},{16,14},{18,16},{20... | collective-permute-start | bytes 884744 | tf_op jit(solution)/shard_map/ppermute | solution.py:21
  52.6 3.2 %copy-start.3 = (bf16[512,4,128]{0,2,1:T(8,128)(2,1)S(1)}, bf16[512,4,128]{0,2,1:T(8,128)(2,1)}, u32[]{:S(2)}) copy-start(bf16[512,4,128]{0,2,1:T(8,128)(2,1)} %copy-done.2) | copy-start | bytes 1572868
  57.2 2.3 %slice-start = ((s8[7077888]{0:T(1024)(128)(4,1)}), s8[4194304]{0:T(1024)(128)(4,1)S(1)}, s32[]{:S(2)}) async-start(s8[7077888]{0:T(1024)(128)(4,1)} %bitcast.441), calls=%async_computation | async-start | bytes 8388608
  58.3 1.2 copy-start.13
  58.6 2.0 %slice-start.1 = ((s8[7077888]{0:T(1024)(128)(4,1)}), s8[2883584]{0:T(1024)(128)(4,1)S(1)}, s32[]{:S(2)}) async-start(s8[7077888]{0:T(1024)(128)(4,1)} %bitcast.441), calls=%async_computation.1 | async-start | bytes 5767168
  77.6 4.8 %copy-start.5 = (bf16[128,3,9,128]{3,0,2,1:T(8,128)(2,1)S(1)}, bf16[128,3,9,128]{3,0,2,1:T(8,128)(2,1)}, u32[]{:S(2)}) copy-start(bf16[128,3,9,128]{3,0,2,1:T(8,128)(2,1)} %slice.345) | copy-start | bytes 2654212
  85.6 1.0 copy-start.6
  87.3 8.6 %collective-permute-start.2 = (bf16[256,4,128]{0,2,1:T(8,128)(2,1)}, bf16[256,4,128]{0,2,1:T(8,128)(2,1)}, u32[]{:S(2)}, u32[]{:S(2)}) collective-permute-start(bf16[256,4,128]{0,2,1:T(8,128)(2,1)} %fusion.110), channel_id=1, source_target_pairs={{0,1},{1,0},{2,3},{3,2},{4,5},{5,4},{6,7},{7,6},{8,9},{9,8},{10,11... | collective-permute-start | bytes 786440 | tf_op jit(solution)/shard_map/ppermute | solution.py:134
  116.2 3.2 %collective-permute-start.4 = (bf16[256,2,128]{0,2,1:T(8,128)(2,1)S(1)}, bf16[256,2,128]{0,2,1:T(8,128)(2,1)S(1)}, u32[]{:S(2)}, u32[]{:S(2)}) collective-permute-start(bf16[256,2,128]{0,2,1:T(8,128)(2,1)S(1)} %slice.378), channel_id=1, source_target_pairs={{2,0},{4,2},{6,4},{8,6},{10,8},{12,10},{14,12},{16,14},{18,16},{20... | collective-permute-start | bytes 393224 | tf_op jit(solution)/shard_map/ppermute | solution.py:21
  119.5 2.2 %slice-start.2 = ((s8[7077888]{0:T(1024)(128)(4,1)}), s8[4194304]{0:T(1024)(128)(4,1)S(1)}, s32[]{:S(2)}) async-start(s8[7077888]{0:T(1024)(128)(4,1)} %bitcast.443), calls=%async_computation.2 | async-start | bytes 8388608
  120.2 2.6 %slice-start.3 = ((s8[7077888]{0:T(1024)(128)(4,1)}), s8[2883584]{0:T(1024)(128)(4,1)S(1)}, s32[]{:S(2)}) async-start(s8[7077888]{0:T(1024)(128)(4,1)} %bitcast.443), calls=%async_computation.3 | async-start | bytes 5767168
  122.8 7.1 %copy-start.8 = (f32[512]{0:T(512)S(1)}, f32[512]{0:T(512)}, u32[]{:S(2)}) copy-start(f32[512]{0:T(512)} %param.11) | copy-start | bytes 6148
  122.8 7.8 %copy-start.10 = (f32[32]{0:T(128)S(1)}, f32[32]{0:T(128)}, u32[]{:S(2)}) copy-start(f32[32]{0:T(128)} %copy-done.9) | copy-start | bytes 388
  126.6 1.0 copy-start.7
  128.3 7.2 %collective-permute-start.5 = (bf16[256,4,128]{0,2,1:T(8,128)(2,1)}, bf16[256,4,128]{0,2,1:T(8,128)(2,1)}, u32[]{:S(2)}, u32[]{:S(2)}) collective-permute-start(bf16[256,4,128]{0,2,1:T(8,128)(2,1)} %fusion.111), channel_id=1, source_target_pairs={{0,1},{1,0},{2,3},{3,2},{4,5},{5,4},{6,7},{7,6},{8,9},{9,8},{10,11... | collective-permute-start | bytes 786440 | tf_op jit(solution)/shard_map/ppermute | solution.py:134

commit v2 on v0

v2 whole, which is shorter than its diff:
```python
import functools

import jax
import jax.numpy as jnp
import numpy as np
from jax import lax
from jax.experimental import pallas as pl
from jax.experimental.pallas import tpu as pltpu
from jax.sharding import PartitionSpec as P

GROUPS = 32
H1 = 8
W1 = 16
CELLS = H1 * W1
EPS = 1e-06
MESH = pl.DeviceIdType.MESH
F32 = jnp.float32
BF16 = jnp.bfloat16
NT = (((1,), (1,)), ((), ()))


def pooling():
    row = np.arange(3 * (2 * H1 + 1) * W1)
    kx, q = row // ((2 * H1 + 1) * W1), row % ((2 * H1 + 1) * W1)
    odd = q >= CELLS
    y0 = np.where(odd, 2 * (q // W1 - H1) - 1, 2 * (q // W1))
    x0 = 2 * (q % W1) + 1 - kx
    fine = np.arange(4 * CELLS)
    down = fine[None] // (2 * W1) - y0[:, None]
    across = fine[None] % (2 * W1) - x0[:, None]
    hit = (down >= 0) & (down <= 1) & (across >= 0) & (across <= 1)
    return jnp.asarray(hit.astype(np.float32), dtype=BF16)


def sigmoid(values):
    return 1.0 / (1.0 + jnp.exp(-values))


def kernel(
    n, frames,
    x_ref, wt_ref, pool_ref, g1_ref, s1_ref, b1_ref, g2_ref, s2_ref, w1_hbm, w2_hbm,
    out_ref,
    w1, w2, fo, hm, ho, wh, even, odd, p2_send, p2_recv, act, hid, low, grad, gh, p1_send, p1_recv,
    acc, stat, slots, tot1, part1,
    load_sem, send_sem, recv_sem, st_send, st_recv,
):
    me = lax.axis_index("tm")
    ch = lax.axis_index("chan")
    oc = 1 - ch
    rows = frames * CELLS
    half = x_ref.shape[1]
    blocks = half // 128
    per_group = 2 * half // GROUPS
    after, before = lax.rem(me + 1, n), lax.rem(me + n - 1, n)
    mine = pl.ds(pl.multiple_of(ch * half, half), half)
    other = pl.ds(pl.multiple_of(oc * half, half), half)

    load2 = pltpu.make_async_copy(w2_hbm, w2, load_sem.at[0])
    load1 = pltpu.make_async_copy(w1_hbm, w1, load_sem.at[1])
    load2.start()
    load1.start()

    barrier = pltpu.get_barrier_semaphore()
    for k in range(1, n):
        pl.semaphore_signal(
            barrier, inc=1, device_id={"tm": lax.rem(me + k, n)}, device_id_type=MESH
        )
    pl.semaphore_signal(barrier, inc=1, device_id={"chan": oc}, device_id_type=MESH)
    pl.semaphore_signal(barrier, inc=1, device_id={"tm": before, "chan": oc}, device_id_type=MESH)
    pl.semaphore_wait(barrier, n + 1)

    def send(index, src, dst, device):
        return pltpu.make_async_remote_copy(
            src_ref=src, dst_ref=dst, send_sem=send_sem.at[index], recv_sem=recv_sem.at[index],
            device_id=device, device_id_type=MESH,
        )

    def sums(index):
        return [
            pltpu.make_async_remote_copy(
                src_ref=stat.at[index], dst_ref=slots.at[index, k],
                send_sem=st_send.at[index, k], recv_sem=st_recv.at[index, k],
                device_id={"tm": lax.rem(me + k, n)}, device_id_type=MESH,
            )
            for k in range(1, n)
        ]

    def start_sums(index, first, second):
        pieces = [v[:, 128 * i : 128 * i + 128] for v in (first, second) for i in range(blocks)]
        pieces.append(jnp.zeros((8 - len(pieces), 128), F32))
        stat[index] = jnp.concatenate(pieces, axis=0)
        copies = sums(index)
        for copy in copies:
            copy.start()
        return copies

    def finish_sums(index, copies):
        for copy in copies:
            copy.wait()
        total = stat[index]
        for k in range(1, n):
            total = total + slots[index, k]
        return total

    in_group = (
        lax.broadcasted_iota(jnp.int32, (half, half), 0) // per_group
        == lax.broadcasted_iota(jnp.int32, (half, half), 1) // per_group
    ).astype(F32)
    count = per_group * rows * n

    def group_means(total):
        first = jnp.concatenate([total[i : i + 1] for i in range(blocks)], axis=1)
        second = jnp.concatenate([total[blocks + i : blocks + i + 1] for i in range(blocks)], axis=1)
        both = jnp.concatenate([first, second, jnp.zeros((6, half), F32)], axis=0)
        spread = jnp.dot(
            both, in_group, precision=lax.Precision.HIGHEST, preferred_element_type=F32
        ) / count
        return spread[0:1], spread[1:2]

    def norm_of(total):
        mean, square = group_means(total)
        return mean, lax.rsqrt(square - mean * mean + EPS)

    def frame(ref, t):
        return ref[t * CELLS : (t + 1) * CELLS, :]

    features = send(0, x_ref, fo, {"chan": oc})
    tail = x_ref.at[pl.ds(rows - 2 * CELLS, 2 * CELLS)]
    halo_mine = send(1, tail, hm, {"tm": after})
    halo_other = send(2, tail, ho, {"tm": after, "chan": oc})
    halo_cot = send(3, wt_ref.at[pl.ds(0, 2)], wh, {"tm": before})
    features.start()
    halo_cot.start()
    halo_mine.start()
    halo_other.start()

    first = jnp.zeros((1, half), F32)
    second = jnp.zeros((1, half), F32)
    for t in range(frames):
        values = frame(x_ref, t).astype(F32)
        first = first + jnp.sum(values, axis=0, keepdims=True)
        second = second + jnp.sum(values * values, axis=0, keepdims=True)
    copies1 = start_sums(0, first, second)

    span = (2 * H1 + 1) * W1
    lanes = wt_ref.shape[2]

    def pooled(values):
        return jnp.dot(pool_ref[...], values, preferred_element_type=F32)

    def keep(ref, t, values):
        for kx in range(3):
            ref[t, :, kx * lanes : (kx + 1) * lanes] = values[kx * span : (kx + 1) * span].astype(BF16)

    def pair(t, _):
        one = pooled(wt_ref[2 * t])
        two = pooled(wt_ref[2 * t + 1])
        keep(even, t, one + two)
        return 0

    lax.fori_loop(0, frames, pair, 0)

    def pair_odd(t, _):
        keep(odd, t, pooled(wt_ref[2 * t + 1]) + pooled(wt_ref[2 * t + 2]))
        return 0

    lax.fori_loop(0, frames - 1, pair_odd, 0)
    halo_cot.wait()
    more = jnp.where(me < n - 1, 1.0, 0.0)
    one = pooled(wh[0]) * more
    two = pooled(wh[1]) * more
    keep(even, frames, one + two)
    keep(odd, frames - 1, pooled(wt_ref[2 * frames - 1]) + one)

    tot1[...] = finish_sums(0, copies1)
    partner = send(4, tot1, part1, {"chan": oc})
    partner.start()

    def conv_two(which):
        acc[...] = jnp.zeros_like(acc)
        for kt in range(3):
            source, t0 = ((even, 1), (odd, 0), (even, 0))[kt]
            for ky in range(3):
                start = (CELLS + W1, 0, CELLS)[ky]
                left = source[t0 : t0 + frames, start : start + CELLS, :].reshape(rows, 3 * lanes)
                tap = 9 * kt + 3 * ky
                right = jnp.concatenate([w2[tap + kx, which, :] for kx in range(3)], axis=1)
                acc[...] += lax.dot_general(left, right, NT, preferred_element_type=F32)

    load2.wait()
    conv_two(other)
    p2_send[...] = acc[...].astype(BF16)
    exchange2 = send(5, p2_send, p2_recv, {"chan": oc})
    exchange2.start()

    cell = lax.broadcasted_iota(jnp.int32, (CELLS, CELLS), 0)
    source = lax.broadcasted_iota(jnp.int32, (CELLS, CELLS), 1)
    left_of = ((source == cell - 1) & (cell % W1 > 0)).astype(F32).astype(BF16)
    right_of = ((source == cell + 1) & (cell % W1 < W1 - 1)).astype(F32).astype(BF16)

    def shifted(values):
        return (
            jnp.dot(left_of, values, preferred_element_type=F32).astype(BF16),
            values,
            jnp.dot(right_of, values, preferred_element_type=F32).astype(BF16),
        )

    inside = slice(W1, W1 + CELLS)
    for ref in (act, grad):
        edge = jnp.zeros((frames + 2, W1, ref.shape[2]), BF16)
        ref[:, :W1, :] = edge
        ref[:, W1 + CELLS :, :] = edge

    partner.wait()
    mean1, inv1 = norm_of(tot1[...])
    mean_o, inv_o = norm_of(part1[...])
    gain1, shift1 = g1_ref[:, mine], s1_ref[:, mine]

    def activate(values, mean, inv, which):
        pre = (values.astype(F32) - mean) * inv * g1_ref[:, which] + s1_ref[:, which]
        return pre * sigmoid(pre)

    def place(t, values, index):
        for kx, moved in enumerate(shifted(values)):
            where = pl.ds(pl.multiple_of(kx * 2 * half + index * half, half), half)
            act[t, inside, where] = moved

    for t in range(frames):
        place(t + 2, activate(frame(x_ref, t), mean1, inv1, mine).astype(BF16), ch)
    halo_mine.wait()
    started = jnp.where(me > 0, 1.0, 0.0)
    for t in range(2):
        place(t, (activate(frame(hm, t), mean1, inv1, mine) * started).astype(BF16), ch)
    features.wait()
    for t in range(frames):
        place(t + 2, activate(frame(fo, t), mean_o, inv_o, other).astype(BF16), oc)
    halo_other.wait()
    for t in range(2):
        place(t, (activate(frame(ho, t), mean_o, inv_o, other) * started).astype(BF16), oc)

    load1.wait()
    acc[...] = jnp.zeros_like(acc)

    def forward(kt, _):
        for ky in range(3):
            left = act[pl.ds(kt, frames), ky * W1 : ky * W1 + CELLS, :].reshape(rows, 6 * half)
            right = w1[pl.ds(9 * kt + 3 * ky, 3)].reshape(6 * half, half)
            acc[...] += jnp.dot(left, right, preferred_element_type=F32)
        return 0

    lax.fori_loop(0, 3, forward, 0)
    first = jnp.zeros((1, half), F32)
    second = jnp.zeros((1, half), F32)
    for t in range(frames):
        values = (frame(acc, t) + b1_ref[...]).astype(BF16)
        hid[t * CELLS : (t + 1) * CELLS, :] = values
        values = values.astype(F32)
        first = first + jnp.sum(values, axis=0, keepdims=True)
        second = second + jnp.sum(values * values, axis=0, keepdims=True)
    copies2 = start_sums(1, first, second)
    conv_two(mine)
    exchange2.wait()

    mean2, inv2 = norm_of(finish_sums(1, copies2))
    gain2, shift2 = g2_ref[:, mine], s2_ref[:, mine]

    def slope(pre):
        sig = sigmoid(pre)
        return sig * (1.0 + pre * (1.0 - sig))

    first = jnp.zeros((1, half), F32)
    second = jnp.zeros((1, half), F32)
    for t in range(frames):
        norm = (frame(hid, t).astype(F32) - mean2) * inv2
        block = frame(acc, t) + frame(p2_recv, t).astype(F32)
        values = block * (slope(norm * gain2 + shift2) * gain2)
        low[t * CELLS : (t + 1) * CELLS, :] = values
        first = first + jnp.sum(values, axis=0, keepdims=True)
        second = second + jnp.sum(values * norm, axis=0, keepdims=True)
    copies3 = start_sums(2, first, second)
    m1, m2 = group_means(finish_sums(2, copies3))

    def put(t, values):
        moved = shifted(values)
        for kx in range(3):
            grad[t, inside, kx * half : (kx + 1) * half] = moved[2 - kx]

    def hidden_grad(t):
        norm = (frame(hid, t).astype(F32) - mean2) * inv2
        return ((frame(low, t) - m1 - norm * m2) * inv2).astype(BF16)

    for t in range(2):
        gh[t] = hidden_grad(t)
    halo_grad = send(6, gh.at[pl.ds(0, 2)], gh.at[pl.ds(2, 2)], {"tm": before})
    halo_grad.start()
    for t in range(frames):
        put(t, gh[t] if t < 2 else hidden_grad(t))

    def back(kt, which):
        for ky in range(3):
            y0 = (2 - ky) * W1
            left = grad[pl.ds(2 - kt, frames), y0 : y0 + CELLS, :].reshape(rows, 3 * half)
            tap = 9 * kt + 3 * ky
            right = jnp.concatenate([w1[tap + kx, which, :] for kx in range(3)], axis=1)
            acc[...] += lax.dot_general(left, right, NT, preferred_element_type=F32)

    acc[...] = jnp.zeros_like(acc)
    back(2, other)
    halo_grad.wait()
    for t in range(2):
        put(frames + t, (gh[2 + t].astype(F32) * more).astype(BF16))
    lax.fori_loop(0, 2, lambda kt, _: (back(kt, other), 0)[1], 0)
    p1_send[...] = acc[...].astype(BF16)
    exchange1 = send(7, p1_send, p1_recv, {"chan": oc})
    exchange1.start()
    acc[...] = jnp.zeros_like(acc)
    lax.fori_loop(0, 3, lambda kt, _: (back(kt, mine), 0)[1], 0)
    exchange1.wait()

    first = jnp.zeros((1, half), F32)
    second = jnp.zeros((1, half), F32)
    for t in range(frames):
        norm = (frame(x_ref, t).astype(F32) - mean1) * inv1
        values = frame(acc, t) + frame(p1_recv, t).astype(F32)
        values = values * slope(norm * gain1 + shift1) * gain1
        low[t * CELLS : (t + 1) * CELLS, :] = values
        first = first + jnp.sum(values, axis=0, keepdims=True)
        second = second + jnp.sum(values * norm, axis=0, keepdims=True)
    copies4 = start_sums(3, first, second)
    m1, m2 = group_means(finish_sums(3, copies4))
    for t in range(frames):
        norm = (frame(x_ref, t).astype(F32) - mean1) * inv1
        values = (frame(low, t) - m1 - norm * m2) * inv1
        out_ref[t * CELLS : (t + 1) * CELLS, :] = values.astype(BF16)


def body(
    features, gain_one, shift_one, conv_one, bias_one, gain_two, shift_two, conv_two, cotangent,
    frame_weight,
):
    half, frames, cells = features.shape
    outs = cotangent.shape[0]
    n = lax.axis_size("tm")
    rows = frames * cells
    across = jnp.transpose(features, (1, 2, 0)).reshape(rows, half)
    scale = frame_weight.astype(F32) / 4.0
    weighted = (cotangent.astype(F32) * scale[None, :, None]).astype(BF16)
    weighted = jnp.transpose(weighted, (1, 2, 0))
    pool = pooling()
    span = pool.shape[0] // 3
    vmem = pl.BlockSpec(memory_space=pltpu.VMEM)
    hbm = pl.BlockSpec(memory_space=pl.ANY)
    out = pl.pallas_call(
        functools.partial(kernel, n, frames),
        out_shape=jax.ShapeDtypeStruct((rows, half), BF16),
        in_specs=[vmem] * 8 + [hbm] * 2,
        out_specs=vmem,
        scratch_shapes=[
            pltpu.VMEM(conv_one.shape, BF16),
            pltpu.VMEM(conv_two.shape, BF16),
            pltpu.VMEM((rows, half), BF16),
            pltpu.VMEM((2 * cells, half), BF16),
            pltpu.VMEM((2 * cells, half), BF16),
            pltpu.VMEM((2, 4 * cells, outs), BF16),
            pltpu.VMEM((frames + 1, span, 3 * outs), BF16),
            pltpu.VMEM((frames, span, 3 * outs), BF16),
            pltpu.VMEM((rows, half), BF16),
            pltpu.VMEM((rows, half), BF16),
            pltpu.VMEM((frames + 2, cells + 2 * W1, 6 * half), BF16),
            pltpu.VMEM((rows, half), BF16),
            pltpu.VMEM((rows, half), F32),
            pltpu.VMEM((frames + 2, cells + 2 * W1, 3 * half), BF16),
            pltpu.VMEM((4, cells, half), BF16),
            pltpu.VMEM((rows, half), BF16),
            pltpu.VMEM((rows, half), BF16),
            pltpu.VMEM((rows, half), F32),
            pltpu.VMEM((4, 8, 128), F32),
            pltpu.VMEM((4, n, 8, 128), F32),
            pltpu.VMEM((8, 128), F32),
            pltpu.VMEM((8, 128), F32),
            pltpu.SemaphoreType.DMA((2,)),
            pltpu.SemaphoreType.DMA((8,)),
            pltpu.SemaphoreType.DMA((8,)),
            pltpu.SemaphoreType.DMA((4, n)),
            pltpu.SemaphoreType.DMA((4, n)),
        ],
        compiler_params=pltpu.CompilerParams(
            collective_id=0, has_side_effects=True, vmem_limit_bytes=48 * 1024 * 1024
        ),
    )(
        across, weighted, pool, gain_one[None], shift_one[None], bias_one[None], gain_two[None],
        shift_two[None], conv_one, conv_two,
    )
    return jnp.transpose(out.reshape(frames, cells, half), (2, 0, 1))


def solution(mesh):
    placed = (
        P("chan", "tm", None),
        P(),
        P(),
        P(None, None, "chan"),
        P("chan"),
        P(),
        P(),
        P(None, None, "chan"),
        P("chan", "tm", None),
        P("tm"),
    )
    return jax.shard_map(
        body, mesh=mesh, in_specs=placed, out_specs=P("chan", "tm", None), check_vma=False
    )
```

time: 302 us -> 62.9 us (0.21)
  blocking collectives: 142 us -> 0 us
  Pallas kernels: 0 us -> 51.5 us
  local copies, waits for them, and re-layouts: 56.2 us -> 8.36 us
  waiting for transfers between devices: 35 us -> 0 us
  matrix products: 30.3 us -> 0 us
  other arithmetic: 20 us -> 2.74 us
  between operations: 14.1 us -> 0.1 us
  starting transfers between devices: 4.15 us -> 0 us
    psum x4 -> x0, blocking collectives: 134 us -> none  [tm_total(): return lax.psum((values[0], values[1]), 'tm')]
    pallas_call x0 -> x1, Pallas kernels: none -> 51.5 us  [body(): pl.pallas_call(functools.partial(kernel, n, frames), out_shape=jax.ShapeD...]
    unnamed x99 -> x19, local copies, waits for them, and re-layouts: 37.2 us -> 4.73 us
    dot_general x3 -> x0, matrix products: 30.3 us -> none  [the longest x2 26.4 us: conv_transpose(): jnp.einsum('kots,kco->cts', stacked, weight, preferred_element_type=jnp.f...]
    reduce_scatter x2 -> x0, waiting for transfers between devices: 30 us -> none  [the longest x1 16.1 us: body(): lax.psum_scatter(conv_transpose(hid_ext, piece, H1, W1), 'chan', scatter_...]
    reduce_sum x12 -> x0, other arithmetic: 9.25 us -> none  [the longest x1 4.82 us: fold_blocks(): return jnp.sum(blocks, axis=(2, 4, 6)).reshape(rows, frames, H1 * W1)]
    all_gather x1 -> x0, blocking collectives: 7.98 us -> none  [body(): whole = lax.all_gather(features, 'chan', axis=0, tiled=True)]
    slice x6 -> x0, local copies, waits for them, and re-layouts: 6.09 us -> none  [the longest x3 6.04 us: spatial_shift(): grid[..., 1 + delta_y:1 + delta_y + height, 1 + delta_x:1 + delta_x + width]]
  transfers between devices with their start and end apart: 5 -> 0, of which waited for: 5 -> 0; matrix products, arithmetic and copies ran while one was open for 4% -> 0% of each run, Pallas kernels for 0% -> 0%
where the time goes in v2:
time: 62.9 us; the launch traced here: 62.7 us
  Pallas kernels  51.5 us (82%)
  local copies, waits for them, and re-layouts  8.36 us (13%)
  other arithmetic  2.74 us (4%)
    pallas_call x1, Pallas kernels, body(): pl.pallas_call(functools.partial(kernel, n, frames), out_shape=jax.ShapeD...  51.5 us
    unnamed x19, local copies, waits for them, and re-layouts  4.73 us
    reshape x1, local copies, waits for them, and re-layouts, body(): return jnp.transpose(out.reshape(frames, cells, half), (2, 0, 1))  1.82 us
    transpose x1, local copies, waits for them, and re-layouts, body(): across = jnp.transpose(features, (1, 2, 0)).reshape(rows, half)  1.81 us
    transpose x1, other arithmetic, body(): weighted = jnp.transpose(weighted, (1, 2, 0))  1.55 us

profile of v2, /device:TPU:0, one launch (start us, length us, event | category | flops | bytes accessed | tf_op | source)
XLA Modules:
  0.0 62.7 jit_solution(13394148897530971388)
XLA Ops:
  0.0 1.2 %convert_multiply_fusion = f32[8]{0:T(128)} fusion(s32[8]{0:T(128)} %param.20), kind=kLoop, calls=%fused_computation.2 | loop fusion | flops 16 | bytes 64 | tf_op jit(solution)/shard_map/div | solution.py:346
  1.2 1.8 %copy.12 = bf16[4,128,256]{2,1,0:T(8,128)(2,1)} copy(bf16[4,128,256]{1,0,2:T(4,128)(2,1)} %bitcast.18) | data formatting | bytes 524288 | tf_op jit(solution)/shard_map/transpose | solution.py:345
  3.0 0.0 copy-start
  3.0 0.0 copy-start.4
  3.0 0.0 copy-start.5
  3.0 0.0 copy-start.6
  3.0 0.0 copy-start.7
  3.0 2.9 %copy.13 = bf16[128,8,512]{0,2,1:T(8,128)(2,1)} copy(bf16[128,8,512]{2,1,0:T(8,128)(2,1)} %param.19) | data formatting | bytes 2097152 | tf_op args[8]
  5.9 0.0 copy-start.1
  5.9 0.0 copy-start.8
  5.9 1.6 %fusion.wt_ref = bf16[8,512,128]{2,1,0:T(8,128)(2,1)S(1)} fusion(bf16[128,8,512]{0,2,1:T(8,128)(2,1)} %copy.13, f32[8]{0:T(128)} %convert_multiply_fusion), kind=kLoop, calls=%fused_computation.1 | loop fusion | flops 1572864 | bytes 2097184 | tf_op jit(solution)/shard_map/transpose | solution.py:348
  7.5 0.0 copy-done
  7.5 0.0 copy-done.4
  7.5 0.0 copy-done.5
  7.5 0.0 copy-done.6
  7.5 0.0 copy-done.7
  7.5 0.0 copy-done.1
  7.5 0.0 copy-done.8
  7.5 0.0 copy-start.3
  7.5 1.1 %copy-done.3 = bf16[816,512]{1,0:T(8,128)(2,1)S(1)} copy-done((bf16[816,512]{1,0:T(8,128)(2,1)S(1)}, bf16[816,512]{1,0:T(8,128)(2,1)}, u32[]{:S(2)}) %copy-start.3) | copy-done | bytes 835608
  8.7 51.5 %shard_map.109 = bf16[512,256]{1,0:T(8,128)(2,1)S(1)} custom-call(bf16[512,256]{1,0:T(8,128)(2,1)S(1)} %bitcast.11, bf16[8,512,128]{2,1,0:T(8,128)(2,1)S(1)} %fusion.wt_ref, bf16[816,512]{1,0:T(8,128)(2,1)S(1)} %copy-done.3, f32[1,512]{1,0:T(1,128)S(1)} %bitcast.13, f32[1,512]{1,0:T(1,128)S(1)} %bitcast.14, f32[1,256]{1,0:T(1,128)S(1)} %bitcast.17, ...), custom_call_target="tpu_custom_call" | custom-call | tf_op jit(solution)/shard_map/pallas_call | solution.py:353
  60.1 0.0 copy-start.2
  60.2 0.7 %copy-done.2 = bf16[512,256]{1,0:T(8,128)(2,1)} copy-done((bf16[512,256]{1,0:T(8,128)(2,1)}, bf16[512,256]{1,0:T(8,128)(2,1)S(1)}, u32[]{:S(2)}) %copy-start.2) | copy-done | bytes 262168
  60.8 1.8 %copy.14 = bf16[4,128,256]{1,0,2:T(4,128)(2,1)} copy(bf16[4,128,256]{2,1,0:T(8,128)(2,1)} %bitcast.12) | data formatting | bytes 524288 | tf_op jit(solution)/shard_map/reshape | solution.py:394
Async XLA Ops:
  3.0 4.5 %copy-start = (bf16[27,512,128]{2,1,0:T(8,128)(2,1)S(1)}, bf16[27,512,128]{2,1,0:T(8,128)(2,1)}, u32[]{:S(2)}) copy-start(bf16[27,512,128]{2,1,0:T(8,128)(2,1)} %w2_hbm.1) | copy-start | bytes 10616836
  3.0 4.5 %copy-start.4 = (f32[512]{0:T(512)S(1)}, f32[512]{0:T(512)}, u32[]{:S(2)}) copy-start(f32[512]{0:T(512)} %param.12) | copy-start | bytes 6148
  3.0 4.5 %copy-start.5 = (f32[512]{0:T(512)S(1)}, f32[512]{0:T(512)}, u32[]{:S(2)}) copy-start(f32[512]{0:T(512)} %param.13) | copy-start | bytes 6148
  3.0 4.5 %copy-start.6 = (f32[512]{0:T(512)S(1)}, f32[512]{0:T(512)}, u32[]{:S(2)}) copy-start(f32[512]{0:T(512)} %param.16) | copy-start | bytes 6148
  3.0 4.5 %copy-start.7 = (f32[512]{0:T(512)S(1)}, f32[512]{0:T(512)}, u32[]{:S(2)}) copy-start(f32[512]{0:T(512)} %param.17) | copy-start | bytes 6148
  5.9 1.6 %copy-start.1 = (bf16[4,128,256]{2,1,0:T(8,128)(2,1)S(1)}, bf16[4,128,256]{2,1,0:T(8,128)(2,1)}, u32[]{:S(2)}) copy-start(bf16[4,128,256]{2,1,0:T(8,128)(2,1)} %copy.12) | copy-start | bytes 786436
  5.9 1.6 %copy-start.8 = (f32[256]{0:T(256)S(1)}, f32[256]{0:T(256)}, u32[]{:S(2)}) copy-start(f32[256]{0:T(256)} %param.15) | copy-start | bytes 3076
  7.5 1.2 %copy-start.3 = (bf16[816,512]{1,0:T(8,128)(2,1)S(1)}, bf16[816,512]{1,0:T(8,128)(2,1)}, u32[]{:S(2)}) copy-start(bf16[816,512]{1,0:T(8,128)(2,1)} %constant.5.clone.pool_ref) | copy-start | bytes 2506756
  60.1 0.7 %copy-start.2 = (bf16[512,256]{1,0:T(8,128)(2,1)}, bf16[512,256]{1,0:T(8,128)(2,1)S(1)}, u32[]{:S(2)}) copy-start(bf16[512,256]{1,0:T(8,128)(2,1)S(1)} %shard_map.109) | copy-start | bytes 786436

commit v3 on v2

--- a/solution.py
+++ b/solution.py
@@ -38,10 +38,10 @@
 
 def kernel(
     n, frames,
-    x_ref, wt_ref, pool_ref, g1_ref, s1_ref, b1_ref, g2_ref, s2_ref, w1_hbm, w2_hbm,
+    x_ref, fw_ref, g1_ref, s1_ref, b1_ref, g2_ref, s2_ref, cot_hbm, pool_hbm, w1_hbm, w2_hbm,
     out_ref,
-    w1, w2, fo, hm, ho, wh, even, odd, p2_send, p2_recv, act, hid, low, grad, gh, p1_send, p1_recv,
-    acc, stat, slots, tot1, part1,
+    cot, fine, wt, pool, prev, w1, w2, fo, hm, ho, wh, even, odd, p2_send, p2_recv, act, hid, low, grad, gh, p1_send, p1_recv,
+    acc, slope_m, slope_o, stat, slots, tot1, part1, tot4, part4,
     load_sem, send_sem, recv_sem, st_send, st_recv,
 ):
     me = lax.axis_index("tm")
@@ -57,6 +57,10 @@
 
     load2 = pltpu.make_async_copy(w2_hbm, w2, load_sem.at[0])
     load1 = pltpu.make_async_copy(w1_hbm, w1, load_sem.at[1])
+    load_cot = pltpu.make_async_copy(cot_hbm, cot, load_sem.at[2])
+    load_pool = pltpu.make_async_copy(pool_hbm, pool, load_sem.at[3])
+    load_cot.start()
+    load_pool.start()
     load2.start()
     load1.start()
 
@@ -67,7 +71,6 @@
         )
     pl.semaphore_signal(barrier, inc=1, device_id={"chan": oc}, device_id_type=MESH)
     pl.semaphore_signal(barrier, inc=1, device_id={"tm": before, "chan": oc}, device_id_type=MESH)
-    pl.semaphore_wait(barrier, n + 1)
 
     def send(index, src, dst, device):
         return pltpu.make_async_remote_copy(
@@ -105,16 +108,18 @@
     in_group = (
         lax.broadcasted_iota(jnp.int32, (half, half), 0) // per_group
         == lax.broadcasted_iota(jnp.int32, (half, half), 1) // per_group
-    ).astype(F32)
+    ).astype(F32).astype(BF16)
     count = per_group * rows * n
 
     def group_means(total):
         first = jnp.concatenate([total[i : i + 1] for i in range(blocks)], axis=1)
         second = jnp.concatenate([total[blocks + i : blocks + i + 1] for i in range(blocks)], axis=1)
         both = jnp.concatenate([first, second, jnp.zeros((6, half), F32)], axis=0)
-        spread = jnp.dot(
-            both, in_group, precision=lax.Precision.HIGHEST, preferred_element_type=F32
-        ) / count
+        high = both.astype(BF16).astype(F32)
+        middle = (both - high).astype(BF16).astype(F32)
+        parts = jnp.concatenate([high, middle, both - high - middle, jnp.zeros_like(both)], axis=0)
+        spread = jnp.dot(parts.astype(BF16), in_group, preferred_element_type=F32)
+        spread = (spread[0:8] + spread[8:16] + spread[16:24]) / count
         return spread[0:1], spread[1:2]
 
     def norm_of(total):
@@ -128,49 +133,64 @@
     tail = x_ref.at[pl.ds(rows - 2 * CELLS, 2 * CELLS)]
     halo_mine = send(1, tail, hm, {"tm": after})
     halo_other = send(2, tail, ho, {"tm": after, "chan": oc})
-    halo_cot = send(3, wt_ref.at[pl.ds(0, 2)], wh, {"tm": before})
-    features.start()
-    halo_cot.start()
-    halo_mine.start()
-    halo_other.start()
-
+    halo_cot = send(3, wt.at[pl.ds(0, 2)], wh, {"tm": before})
     first = jnp.zeros((1, half), F32)
     second = jnp.zeros((1, half), F32)
     for t in range(frames):
         values = frame(x_ref, t).astype(F32)
         first = first + jnp.sum(values, axis=0, keepdims=True)
         second = second + jnp.sum(values * values, axis=0, keepdims=True)
+
+    pl.semaphore_wait(barrier, n + 1)
+    features.start()
+    halo_mine.start()
     copies1 = start_sums(0, first, second)
+    halo_other.start()
 
     span = (2 * H1 + 1) * W1
-    lanes = wt_ref.shape[2]
-
-    def pooled(values):
-        return jnp.dot(pool_ref[...], values, preferred_element_type=F32)
+    fast = 2 * frames
+    lanes = wt.shape[1]
+    frame_row = lax.broadcasted_iota(jnp.int32, (fast, 1), 0)
+    scale = jnp.zeros((fast, 1), F32)
+    for t in range(fast):
+        scale = jnp.where(frame_row == t, fw_ref[t].astype(F32) / 4.0, scale)
+    load_cot.wait()
+    chunk = 16 * fast
+    for i in range(lanes // 16):
+        where = slice(i * chunk, (i + 1) * chunk)
+        values = cot[where, :].astype(F32).reshape(16, fast, 4 * CELLS) * scale[None]
+        values = values.reshape(chunk, 4 * CELLS)
+        for j in range(4 * CELLS // 128):
+            fine[j, where, :] = values[:, 128 * j : 128 * j + 128]
+    for t in range(fast):
+        for j in range(4 * CELLS // 128):
+            values = fine[j, pl.ds(t, lanes, stride=fast), :]
+            wt[t, :, 128 * j : 128 * j + 128] = values.astype(BF16)
+        if t == 1:
+            halo_cot.start()
 
     def keep(ref, t, values):
         for kx in range(3):
             ref[t, :, kx * lanes : (kx + 1) * lanes] = values[kx * span : (kx + 1) * span].astype(BF16)
 
-    def pair(t, _):
-        one = pooled(wt_ref[2 * t])
-        two = pooled(wt_ref[2 * t + 1])
+    def pooled(values):
+        both = lax.dot_general(
+            pool[...], values.reshape(2 * lanes, 4 * CELLS), NT, preferred_element_type=F32
+        )
+        return both[:, :lanes], both[:, lanes:]
+
+    load_pool.wait()
+    for t in range(frames):
+        one, two = pooled(wt[2 * t : 2 * t + 2])
         keep(even, t, one + two)
-        return 0
-
-    lax.fori_loop(0, frames, pair, 0)
-
-    def pair_odd(t, _):
-        keep(odd, t, pooled(wt_ref[2 * t + 1]) + pooled(wt_ref[2 * t + 2]))
-        return 0
-
-    lax.fori_loop(0, frames - 1, pair_odd, 0)
+        if t > 0:
+            keep(odd, t - 1, prev[...] + one)
+        prev[...] = two
     halo_cot.wait()
     more = jnp.where(me < n - 1, 1.0, 0.0)
-    one = pooled(wh[0]) * more
-    two = pooled(wh[1]) * more
-    keep(even, frames, one + two)
-    keep(odd, frames - 1, pooled(wt_ref[2 * frames - 1]) + one)
+    one, two = pooled(wh[...])
+    keep(even, frames, (one + two) * more)
+    keep(odd, frames - 1, prev[...] + one * more)
 
     tot1[...] = finish_sums(0, copies1)
     partner = send(4, tot1, part1, {"chan": oc})
@@ -278,6 +298,18 @@
         first = first + jnp.sum(values, axis=0, keepdims=True)
         second = second + jnp.sum(values * norm, axis=0, keepdims=True)
     copies3 = start_sums(2, first, second)
+
+    def norm_one(t):
+        return (frame(x_ref, t).astype(F32) - mean1) * inv1
+
+    def norm_other(t):
+        return (frame(fo, t).astype(F32) - mean_o) * inv_o
+
+    gain_o, shift_o = g1_ref[:, other], s1_ref[:, other]
+    for t in range(frames):
+        part = slice(t * CELLS, (t + 1) * CELLS)
+        slope_m[part, :] = slope(norm_one(t) * gain1 + shift1) * gain1
+        slope_o[part, :] = slope(norm_other(t) * gain_o + shift_o) * gain_o
     m1, m2 = group_means(finish_sums(2, copies3))
 
     def put(t, values):
@@ -313,24 +345,30 @@
     p1_send[...] = acc[...].astype(BF16)
     exchange1 = send(7, p1_send, p1_recv, {"chan": oc})
     exchange1.start()
+
+    def slope_sums(slopes, norm_at):
+        first = jnp.zeros((1, half), F32)
+        second = jnp.zeros((1, half), F32)
+        for t in range(frames):
+            values = frame(acc, t) * frame(slopes, t)
+            first = first + jnp.sum(values, axis=0, keepdims=True)
+            second = second + jnp.sum(values * norm_at(t), axis=0, keepdims=True)
+        return first, second
+
+    copies4 = start_sums(3, *slope_sums(slope_o, norm_other))
     acc[...] = jnp.zeros_like(acc)
     lax.fori_loop(0, 3, lambda kt, _: (back(kt, mine), 0)[1], 0)
+    copies5 = start_sums(4, *slope_sums(slope_m, norm_one))
+    tot4[...] = finish_sums(3, copies4)
+    partner4 = send(8, tot4, part4, {"chan": oc})
+    partner4.start()
+    total = finish_sums(4, copies5)
+    partner4.wait()
+    m1, m2 = group_means(total + part4[...])
     exchange1.wait()
-
-    first = jnp.zeros((1, half), F32)
-    second = jnp.zeros((1, half), F32)
-    for t in range(frames):
-        norm = (frame(x_ref, t).astype(F32) - mean1) * inv1
-        values = frame(acc, t) + frame(p1_recv, t).astype(F32)
-        values = values * slope(norm * gain1 + shift1) * gain1
-        low[t * CELLS : (t + 1) * CELLS, :] = values
-        first = first + jnp.sum(values, axis=0, keepdims=True)
-        second = second + jnp.sum(values * norm, axis=0, keepdims=True)
-    copies4 = start_sums(3, first, second)
-    m1, m2 = group_means(finish_sums(3, copies4))
-    for t in range(frames):
-        norm = (frame(x_ref, t).astype(F32) - mean1) * inv1
-        values = (frame(low, t) - m1 - norm * m2) * inv1
+    for t in range(frames):
+        values = (frame(acc, t) + frame(p1_recv, t).astype(F32)) * frame(slope_m, t)
+        values = (values - m1 - norm_one(t) * m2) * inv1
         out_ref[t * CELLS : (t + 1) * CELLS, :] = values.astype(BF16)
 
 
@@ -343,9 +381,7 @@
     n = lax.axis_size("tm")
     rows = frames * cells
     across = jnp.transpose(features, (1, 2, 0)).reshape(rows, half)
-    scale = frame_weight.astype(F32) / 4.0
-    weighted = (cotangent.astype(F32) * scale[None, :, None]).astype(BF16)
-    weighted = jnp.transpose(weighted, (1, 2, 0))
+    fine = cotangent.reshape(outs * cotangent.shape[1], cotangent.shape[2])
     pool = pooling()
     span = pool.shape[0] // 3
     vmem = pl.BlockSpec(memory_space=pltpu.VMEM)
@@ -353,15 +389,20 @@
     out = pl.pallas_call(
         functools.partial(kernel, n, frames),
         out_shape=jax.ShapeDtypeStruct((rows, half), BF16),
-        in_specs=[vmem] * 8 + [hbm] * 2,
+        in_specs=[vmem, pl.BlockSpec(memory_space=pltpu.SMEM)] + [vmem] * 5 + [hbm] * 4,
         out_specs=vmem,
         scratch_shapes=[
+            pltpu.VMEM(fine.shape, BF16),
+            pltpu.VMEM((4 * cells // 128, fine.shape[0], 128), F32),
+            pltpu.VMEM((2 * frames, outs, 4 * cells), BF16),
+            pltpu.VMEM(pool.shape, BF16),
+            pltpu.VMEM((pool.shape[0], outs), F32),
             pltpu.VMEM(conv_one.shape, BF16),
             pltpu.VMEM(conv_two.shape, BF16),
             pltpu.VMEM((rows, half), BF16),
             pltpu.VMEM((2 * cells, half), BF16),
             pltpu.VMEM((2 * cells, half), BF16),
-            pltpu.VMEM((2, 4 * cells, outs), BF16),
+            pltpu.VMEM((2, outs, 4 * cells), BF16),
             pltpu.VMEM((frames + 1, span, 3 * outs), BF16),
             pltpu.VMEM((frames, span, 3 * outs), BF16),
             pltpu.VMEM((rows, half), BF16),
@@ -374,22 +415,26 @@
             pltpu.VMEM((rows, half), BF16),
             pltpu.VMEM((rows, half), BF16),
             pltpu.VMEM((rows, half), F32),
-            pltpu.VMEM((4, 8, 128), F32),
-            pltpu.VMEM((4, n, 8, 128), F32),
+            pltpu.VMEM((rows, half), F32),
+            pltpu.VMEM((rows, half), F32),
+            pltpu.VMEM((5, 8, 128), F32),
+            pltpu.VMEM((5, n, 8, 128), F32),
             pltpu.VMEM((8, 128), F32),
             pltpu.VMEM((8, 128), F32),
-            pltpu.SemaphoreType.DMA((2,)),
-            pltpu.SemaphoreType.DMA((8,)),
-            pltpu.SemaphoreType.DMA((8,)),
-            pltpu.SemaphoreType.DMA((4, n)),
-            pltpu.SemaphoreType.DMA((4, n)),
+            pltpu.VMEM((8, 128), F32),
+            pltpu.VMEM((8, 128), F32),
+            pltpu.SemaphoreType.DMA((4,)),
+            pltpu.SemaphoreType.DMA((9,)),
+            pltpu.SemaphoreType.DMA((9,)),
+            pltpu.SemaphoreType.DMA((5, n)),
+            pltpu.SemaphoreType.DMA((5, n)),
         ],
         compiler_params=pltpu.CompilerParams(
-            collective_id=0, has_side_effects=True, vmem_limit_bytes=48 * 1024 * 1024
+            collective_id=0, has_side_effects=True, vmem_limit_bytes=56 * 1024 * 1024
         ),
     )(
-        across, weighted, pool, gain_one[None], shift_one[None], bias_one[None], gain_two[None],
-        shift_two[None], conv_one, conv_two,
+        across, frame_weight, gain_one[None], shift_one[None], bias_one[None], gain_two[None],
+        shift_two[None], fine, pool, conv_one, conv_two,
     )
     return jnp.transpose(out.reshape(frames, cells, half), (2, 0, 1))
 

time: 62.9 us -> 53.3 us (0.85)
  local copies, waits for them, and re-layouts: 8.36 us -> 3.63 us
  other arithmetic: 2.74 us -> 0 us
  Pallas kernels: 51.5 us -> 49.5 us
    unnamed x19 -> x0, local copies, waits for them, and re-layouts: 4.73 us -> none
    pallas_call x1, Pallas kernels: 51.5 us -> 49.5 us  [body(): pl.pallas_call(functools.partial(kernel, n, frames), out_shape=jax.ShapeD...]
    transpose x1 -> x0, other arithmetic: 1.55 us -> none  [body(): weighted = jnp.transpose(weighted, (1, 2, 0))]
    div x1 -> x0, other arithmetic: 1.18 us -> none  [body(): scale = frame_weight.astype(F32) / 4.0]
where the time goes in v3:
time: 53.3 us; the launch traced here: 53.2 us
  Pallas kernels  49.5 us (93%)
  local copies, waits for them, and re-layouts  3.63 us (7%)
    pallas_call x1, Pallas kernels, body(): pl.pallas_call(functools.partial(kernel, n, frames), out_shape=jax.ShapeD...  49.5 us
    reshape x1, local copies, waits for them, and re-layouts, body(): return jnp.transpose(out.reshape(frames, cells, half), (2, 0, 1))  1.82 us
    transpose x1, local copies, waits for them, and re-layouts, body(): across = jnp.transpose(features, (1, 2, 0)).reshape(rows, half)  1.81 us

profile of v3, /device:TPU:0, one launch (start us, length us, event | category | flops | bytes accessed | tf_op | source)
XLA Modules:
  0.0 53.2 jit_solution(13027837769086179898)
XLA Ops:
  0.0 1.8 %copy.12 = bf16[4,128,256]{2,1,0:T(8,128)(2,1)} copy(bf16[4,128,256]{1,0,2:T(4,128)(2,1)} %bitcast.13) | data formatting | bytes 524288 | tf_op jit(solution)/shard_map/transpose | solution.py:383
  1.8 49.5 %shard_map.109 = bf16[512,256]{1,0:T(8,128)(2,1)} custom-call(bf16[512,256]{1,0:T(8,128)(2,1)} %bitcast.12, s32[8]{0:T(128)} %fw_ref.1, f32[1,512]{1,0:T(1,128)} %bitcast.14, f32[1,512]{1,0:T(1,128)} %bitcast.15, f32[1,256]{1,0:T(1,128)} %bitcast.18, f32[1,512]{1,0:T(1,128)} %bitcast.16, f32[1,512]{1,0:T(1,128)} %bitcast.17, bf16[1024,512]{1,0:T(8,128)(2,1)} %bitcast.10, ...), custom_call_target="tpu_custom_call" | custom-call | tf_op jit(solution)/shard_map/pallas_call | solution.py:389
  51.3 1.8 %copy.13 = bf16[4,128,256]{1,0,2:T(4,128)(2,1)} copy(bf16[4,128,256]{2,1,0:T(8,128)(2,1)} %bitcast.11) | data formatting | bytes 524288 | tf_op jit(solution)/shard_map/reshape | solution.py:439

commit v4 on v3

--- a/solution.py
+++ b/solution.py
@@ -40,7 +40,7 @@
     n, frames,
     x_ref, fw_ref, g1_ref, s1_ref, b1_ref, g2_ref, s2_ref, cot_hbm, pool_hbm, w1_hbm, w2_hbm,
     out_ref,
-    cot, fine, wt, pool, prev, w1, w2, fo, hm, ho, wh, even, odd, p2_send, p2_recv, act, hid, low, grad, gh, p1_send, p1_recv,
+    cot, fine, wt, pool, prev, w1, w2, fo, hm, ho, wh, even, odd, p2_send, p2_recv, act_m, act_o, hid, low, grad, gh, p1_send, p1_recv,
     acc, slope_m, slope_o, stat, slots, tot1, part1, tot4, part4,
     load_sem, send_sem, recv_sem, st_send, st_recv,
 ):
@@ -70,7 +70,6 @@
             barrier, inc=1, device_id={"tm": lax.rem(me + k, n)}, device_id_type=MESH
         )
     pl.semaphore_signal(barrier, inc=1, device_id={"chan": oc}, device_id_type=MESH)
-    pl.semaphore_signal(barrier, inc=1, device_id={"tm": before, "chan": oc}, device_id_type=MESH)
 
     def send(index, src, dst, device):
         return pltpu.make_async_remote_copy(
@@ -82,24 +81,28 @@
         return [
             pltpu.make_async_remote_copy(
                 src_ref=stat.at[index], dst_ref=slots.at[index, k],
-                send_sem=st_send.at[index, k], recv_sem=st_recv.at[index, k],
+                send_sem=st_send.at[index], recv_sem=st_recv.at[index],
                 device_id={"tm": lax.rem(me + k, n)}, device_id_type=MESH,
             )
             for k in range(1, n)
         ]
 
+    def all_sums(index):
+        block = slots.at[index, pl.ds(1, n - 1)]
+        return pltpu.make_async_remote_copy(
+            src_ref=block, dst_ref=block, send_sem=st_send.at[index], recv_sem=st_recv.at[index],
+            device_id={"tm": after}, device_id_type=MESH,
+        )
+
     def start_sums(index, first, second):
         pieces = [v[:, 128 * i : 128 * i + 128] for v in (first, second) for i in range(blocks)]
         pieces.append(jnp.zeros((8 - len(pieces), 128), F32))
         stat[index] = jnp.concatenate(pieces, axis=0)
-        copies = sums(index)
-        for copy in copies:
+        for copy in sums(index):
             copy.start()
-        return copies
-
-    def finish_sums(index, copies):
-        for copy in copies:
-            copy.wait()
+
+    def finish_sums(index):
+        all_sums(index).wait_recv()
         total = stat[index]
         for k in range(1, n):
             total = total + slots[index, k]
@@ -129,10 +132,12 @@
     def frame(ref, t):
         return ref[t * CELLS : (t + 1) * CELLS, :]
 
-    features = send(0, x_ref, fo, {"chan": oc})
-    tail = x_ref.at[pl.ds(rows - 2 * CELLS, 2 * CELLS)]
+    early, late = pl.ds(0, rows - 2 * CELLS), pl.ds(rows - 2 * CELLS, 2 * CELLS)
+    tail = x_ref.at[late]
+    features_late = send(9, tail, fo.at[late], {"chan": oc})
+    features = send(0, x_ref.at[early], fo.at[early], {"chan": oc})
     halo_mine = send(1, tail, hm, {"tm": after})
-    halo_other = send(2, tail, ho, {"tm": after, "chan": oc})
+    halo_other = send(2, fo.at[late], ho, {"tm": after})
     halo_cot = send(3, wt.at[pl.ds(0, 2)], wh, {"tm": before})
     first = jnp.zeros((1, half), F32)
     second = jnp.zeros((1, half), F32)
@@ -141,11 +146,11 @@
         first = first + jnp.sum(values, axis=0, keepdims=True)
         second = second + jnp.sum(values * values, axis=0, keepdims=True)
 
-    pl.semaphore_wait(barrier, n + 1)
+    pl.semaphore_wait(barrier, n)
+    features_late.start()
+    start_sums(0, first, second)
+    halo_mine.start()
     features.start()
-    halo_mine.start()
-    copies1 = start_sums(0, first, second)
-    halo_other.start()
 
     span = (2 * H1 + 1) * W1
     fast = 2 * frames
@@ -179,6 +184,8 @@
         )
         return both[:, :lanes], both[:, lanes:]
 
+    features_late.wait()
+    halo_other.start()
     load_pool.wait()
     for t in range(frames):
         one, two = pooled(wt[2 * t : 2 * t + 2])
@@ -192,12 +199,58 @@
     keep(even, frames, (one + two) * more)
     keep(odd, frames - 1, prev[...] + one * more)
 
-    tot1[...] = finish_sums(0, copies1)
+    tot1[...] = finish_sums(0)
     partner = send(4, tot1, part1, {"chan": oc})
     partner.start()
 
+    cell = lax.broadcasted_iota(jnp.int32, (CELLS, CELLS), 0)
+    source = lax.broadcasted_iota(jnp.int32, (CELLS, CELLS), 1)
+    left_of = ((source == cell - 1) & (cell % W1 > 0)).astype(F32).astype(BF16)
+    right_of = ((source == cell + 1) & (cell % W1 < W1 - 1)).astype(F32).astype(BF16)
+
+    def shifted(values):
+        return (
+            jnp.dot(left_of, values, preferred_element_type=F32).astype(BF16),
+            values,
+            jnp.dot(right_of, values, preferred_element_type=F32).astype(BF16),
+        )
+
+    inside = slice(W1, W1 + CELLS)
+    for ref in (act_m, act_o, grad):
+        edge = jnp.zeros((frames + 2, W1, ref.shape[2]), BF16)
+        ref[:, :W1, :] = edge
+        ref[:, W1 + CELLS :, :] = edge
+
+    def activate(values, mean, inv, which):
+        pre = (values.astype(F32) - mean) * inv * g1_ref[:, which] + s1_ref[:, which]
+        return pre * sigmoid(pre)
+
+    def place(ref, t, values):
+        for kx, moved in enumerate(shifted(values.astype(BF16))):
+            ref[t, inside, kx * half : (kx + 1) * half] = moved
+
+    def forward(ref, which):
+        for kt in range(3):
+            for ky in range(3):
+                left = ref[kt : kt + frames, ky * W1 : ky * W1 + CELLS, :].reshape(rows, 3 * half)
+                tap = 9 * kt + 3 * ky
+                right = jnp.concatenate([w1[tap + kx, which, :] for kx in range(3)], axis=0)
+                acc[...] += jnp.dot(left, right, preferred_element_type=F32)
+
+    started = jnp.where(me > 0, 1.0, 0.0)
+    mean1, inv1 = norm_of(tot1[...])
+    gain1, shift1 = g1_ref[:, mine], s1_ref[:, mine]
+    acc[...] = jnp.zeros_like(acc)
+    for t in range(frames):
+        place(act_m, t + 2, activate(frame(x_ref, t), mean1, inv1, mine))
+    halo_mine.wait()
+    for t in range(2):
+        place(act_m, t, activate(frame(hm, t), mean1, inv1, mine) * started)
+    load1.wait()
+    forward(act_m, mine)
+
     def conv_two(which):
-        acc[...] = jnp.zeros_like(acc)
+        low[...] = jnp.zeros_like(low)
         for kt in range(3):
             source, t0 = ((even, 1), (odd, 0), (even, 0))[kt]
             for ky in range(3):
@@ -205,70 +258,23 @@
                 left = source[t0 : t0 + frames, start : start + CELLS, :].reshape(rows, 3 * lanes)
                 tap = 9 * kt + 3 * ky
                 right = jnp.concatenate([w2[tap + kx, which, :] for kx in range(3)], axis=1)
-                acc[...] += lax.dot_general(left, right, NT, preferred_element_type=F32)
+                low[...] += lax.dot_general(left, right, NT, preferred_element_type=F32)
 
     load2.wait()
     conv_two(other)
-    p2_send[...] = acc[...].astype(BF16)
+    p2_send[...] = low[...].astype(BF16)
     exchange2 = send(5, p2_send, p2_recv, {"chan": oc})
     exchange2.start()
 
-    cell = lax.broadcasted_iota(jnp.int32, (CELLS, CELLS), 0)
-    source = lax.broadcasted_iota(jnp.int32, (CELLS, CELLS), 1)
-    left_of = ((source == cell - 1) & (cell % W1 > 0)).astype(F32).astype(BF16)
-    right_of = ((source == cell + 1) & (cell % W1 < W1 - 1)).astype(F32).astype(BF16)
-
-    def shifted(values):
-        return (
-            jnp.dot(left_of, values, preferred_element_type=F32).astype(BF16),
-            values,
-            jnp.dot(right_of, values, preferred_element_type=F32).astype(BF16),
-        )
-
-    inside = slice(W1, W1 + CELLS)
-    for ref in (act, grad):
-        edge = jnp.zeros((frames + 2, W1, ref.shape[2]), BF16)
-        ref[:, :W1, :] = edge
-        ref[:, W1 + CELLS :, :] = edge
-
     partner.wait()
-    mean1, inv1 = norm_of(tot1[...])
     mean_o, inv_o = norm_of(part1[...])
-    gain1, shift1 = g1_ref[:, mine], s1_ref[:, mine]
-
-    def activate(values, mean, inv, which):
-        pre = (values.astype(F32) - mean) * inv * g1_ref[:, which] + s1_ref[:, which]
-        return pre * sigmoid(pre)
-
-    def place(t, values, index):
-        for kx, moved in enumerate(shifted(values)):
-            where = pl.ds(pl.multiple_of(kx * 2 * half + index * half, half), half)
-            act[t, inside, where] = moved
-
-    for t in range(frames):
-        place(t + 2, activate(frame(x_ref, t), mean1, inv1, mine).astype(BF16), ch)
-    halo_mine.wait()
-    started = jnp.where(me > 0, 1.0, 0.0)
-    for t in range(2):
-        place(t, (activate(frame(hm, t), mean1, inv1, mine) * started).astype(BF16), ch)
     features.wait()
     for t in range(frames):
-        place(t + 2, activate(frame(fo, t), mean_o, inv_o, other).astype(BF16), oc)
+        place(act_o, t + 2, activate(frame(fo, t), mean_o, inv_o, other))
     halo_other.wait()
     for t in range(2):
-        place(t, (activate(frame(ho, t), mean_o, inv_o, other) * started).astype(BF16), oc)
-
-    load1.wait()
-    acc[...] = jnp.zeros_like(acc)
-
-    def forward(kt, _):
-        for ky in range(3):
-            left = act[pl.ds(kt, frames), ky * W1 : ky * W1 + CELLS, :].reshape(rows, 6 * half)
-            right = w1[pl.ds(9 * kt + 3 * ky, 3)].reshape(6 * half, half)
-            acc[...] += jnp.dot(left, right, preferred_element_type=F32)
-        return 0
-
-    lax.fori_loop(0, 3, forward, 0)
+        place(act_o, t, activate(frame(ho, t), mean_o, inv_o, other) * started)
+    forward(act_o, other)
     first = jnp.zeros((1, half), F32)
     second = jnp.zeros((1, half), F32)
     for t in range(frames):
@@ -277,11 +283,11 @@
         values = values.astype(F32)
         first = first + jnp.sum(values, axis=0, keepdims=True)
         second = second + jnp.sum(values * values, axis=0, keepdims=True)
-    copies2 = start_sums(1, first, second)
+    start_sums(1, first, second)
     conv_two(mine)
     exchange2.wait()
 
-    mean2, inv2 = norm_of(finish_sums(1, copies2))
+    mean2, inv2 = norm_of(finish_sums(1))
     gain2, shift2 = g2_ref[:, mine], s2_ref[:, mine]
 
     def slope(pre):
@@ -292,12 +298,12 @@
     second = jnp.zeros((1, half), F32)
     for t in range(frames):
         norm = (frame(hid, t).astype(F32) - mean2) * inv2
-        block = frame(acc, t) + frame(p2_recv, t).astype(F32)
+        block = frame(low, t) + frame(p2_recv, t).astype(F32)
         values = block * (slope(norm * gain2 + shift2) * gain2)
         low[t * CELLS : (t + 1) * CELLS, :] = values
         first = first + jnp.sum(values, axis=0, keepdims=True)
         second = second + jnp.sum(values * norm, axis=0, keepdims=True)
-    copies3 = start_sums(2, first, second)
+    start_sums(2, first, second)
 
     def norm_one(t):
         return (frame(x_ref, t).astype(F32) - mean1) * inv1
@@ -310,7 +316,7 @@
         part = slice(t * CELLS, (t + 1) * CELLS)
         slope_m[part, :] = slope(norm_one(t) * gain1 + shift1) * gain1
         slope_o[part, :] = slope(norm_other(t) * gain_o + shift_o) * gain_o
-    m1, m2 = group_means(finish_sums(2, copies3))
+    m1, m2 = group_means(finish_sums(2))
 
     def put(t, values):
         moved = shifted(values)
@@ -328,23 +334,38 @@
     for t in range(frames):
         put(t, gh[t] if t < 2 else hidden_grad(t))
 
-    def back(kt, which):
-        for ky in range(3):
-            y0 = (2 - ky) * W1
-            left = grad[pl.ds(2 - kt, frames), y0 : y0 + CELLS, :].reshape(rows, 3 * half)
-            tap = 9 * kt + 3 * ky
-            right = jnp.concatenate([w1[tap + kx, which, :] for kx in range(3)], axis=1)
-            acc[...] += lax.dot_general(left, right, NT, preferred_element_type=F32)
-
-    acc[...] = jnp.zeros_like(acc)
-    back(2, other)
+    def back(t0, count, which):
+        part = pl.ds(t0 * CELLS, count * CELLS)
+        total = jnp.zeros((count * CELLS, half), F32)
+        acc[part, :] = total
+
+        def add(kt, _):
+            for ky in range(3):
+                y0 = (2 - ky) * W1
+                left = grad[pl.ds(t0 + 2 - kt, count), y0 : y0 + CELLS, :]
+                tap = 9 * kt + 3 * ky
+                right = jnp.concatenate([w1[tap + kx, which, :] for kx in range(3)], axis=1)
+                acc[part, :] += lax.dot_general(
+                    left.reshape(count * CELLS, 3 * half), right, NT, preferred_element_type=F32
+                )
+            return 0
+
+        lax.fori_loop(0, 3, add, 0)
+
+    def send_back(index, t0, count):
+        part = pl.ds(t0 * CELLS, count * CELLS)
+        p1_send[part, :] = acc[part, :].astype(BF16)
+        copy = send(index, p1_send.at[part], p1_recv.at[part], {"chan": oc})
+        copy.start()
+        return copy
+
+    back(0, frames - 2, other)
+    exchange1 = [send_back(7, 0, frames - 2)]
     halo_grad.wait()
     for t in range(2):
         put(frames + t, (gh[2 + t].astype(F32) * more).astype(BF16))
-    lax.fori_loop(0, 2, lambda kt, _: (back(kt, other), 0)[1], 0)
-    p1_send[...] = acc[...].astype(BF16)
-    exchange1 = send(7, p1_send, p1_recv, {"chan": oc})
-    exchange1.start()
+    back(frames - 2, 2, other)
+    exchange1.append(send_back(2 + 8, frames - 2, 2))
 
     def slope_sums(slopes, norm_at):
         first = jnp.zeros((1, half), F32)
@@ -355,21 +376,23 @@
             second = second + jnp.sum(values * norm_at(t), axis=0, keepdims=True)
         return first, second
 
-    copies4 = start_sums(3, *slope_sums(slope_o, norm_other))
-    acc[...] = jnp.zeros_like(acc)
-    lax.fori_loop(0, 3, lambda kt, _: (back(kt, mine), 0)[1], 0)
-    copies5 = start_sums(4, *slope_sums(slope_m, norm_one))
-    tot4[...] = finish_sums(3, copies4)
+    start_sums(3, *slope_sums(slope_o, norm_other))
+    back(0, frames, mine)
+    start_sums(4, *slope_sums(slope_m, norm_one))
+    tot4[...] = finish_sums(3)
     partner4 = send(8, tot4, part4, {"chan": oc})
     partner4.start()
-    total = finish_sums(4, copies5)
+    total = finish_sums(4)
     partner4.wait()
     m1, m2 = group_means(total + part4[...])
-    exchange1.wait()
+    for copy in exchange1:
+        copy.wait()
     for t in range(frames):
         values = (frame(acc, t) + frame(p1_recv, t).astype(F32)) * frame(slope_m, t)
         values = (values - m1 - norm_one(t) * m2) * inv1
         out_ref[t * CELLS : (t + 1) * CELLS, :] = values.astype(BF16)
+    for index in range(5):
+        all_sums(index).wait_send()
 
 
 def body(
@@ -407,7 +430,8 @@
             pltpu.VMEM((frames, span, 3 * outs), BF16),
             pltpu.VMEM((rows, half), BF16),
             pltpu.VMEM((rows, half), BF16),
-            pltpu.VMEM((frames + 2, cells + 2 * W1, 6 * half), BF16),
+            pltpu.VMEM((frames + 2, cells + 2 * W1, 3 * half), BF16),
+            pltpu.VMEM((frames + 2, cells + 2 * W1, 3 * half), BF16),
             pltpu.VMEM((rows, half), BF16),
             pltpu.VMEM((rows, half), F32),
             pltpu.VMEM((frames + 2, cells + 2 * W1, 3 * half), BF16),
@@ -424,10 +448,10 @@
             pltpu.VMEM((8, 128), F32),
             pltpu.VMEM((8, 128), F32),
             pltpu.SemaphoreType.DMA((4,)),
-            pltpu.SemaphoreType.DMA((9,)),
-            pltpu.SemaphoreType.DMA((9,)),
-            pltpu.SemaphoreType.DMA((5, n)),
-            pltpu.SemaphoreType.DMA((5, n)),
+            pltpu.SemaphoreType.DMA((11,)),
+            pltpu.SemaphoreType.DMA((11,)),
+            pltpu.SemaphoreType.DMA((5,)),
+            pltpu.SemaphoreType.DMA((5,)),
         ],
         compiler_params=pltpu.CompilerParams(
             collective_id=0, has_side_effects=True, vmem_limit_bytes=56 * 1024 * 1024

time: 53.3 us -> 54.9 us (1.030)
  Pallas kernels: 49.5 us -> 51 us
    pallas_call x1, Pallas kernels: 49.5 us -> 51 us  [body(): pl.pallas_call(functools.partial(kernel, n, frames), out_shape=jax.ShapeD...]
where the time goes in v4:
time: 54.9 us; the launch traced here: 54.7 us
  Pallas kernels  51 us (93%)
  local copies, waits for them, and re-layouts  3.63 us (7%)
    pallas_call x1, Pallas kernels, body(): pl.pallas_call(functools.partial(kernel, n, frames), out_shape=jax.ShapeD...  51 us
    reshape x1, local copies, waits for them, and re-layouts, body(): return jnp.transpose(out.reshape(frames, cells, half), (2, 0, 1))  1.82 us
    transpose x1, local copies, waits for them, and re-layouts, body(): across = jnp.transpose(features, (1, 2, 0)).reshape(rows, half)  1.81 us

profile of v4, /device:TPU:0, one launch (start us, length us, event | category | flops | bytes accessed | tf_op | source)
XLA Modules:
  0.0 54.7 jit_solution(1693209474895531561)
XLA Ops:
  0.0 1.8 %copy.12 = bf16[4,128,256]{2,1,0:T(8,128)(2,1)} copy(bf16[4,128,256]{1,0,2:T(4,128)(2,1)} %bitcast.13) | data formatting | bytes 524288 | tf_op jit(solution)/shard_map/transpose | solution.py:406
  1.8 51.0 %shard_map.109 = bf16[512,256]{1,0:T(8,128)(2,1)} custom-call(bf16[512,256]{1,0:T(8,128)(2,1)} %bitcast.12, s32[8]{0:T(128)} %fw_ref.1, f32[1,512]{1,0:T(1,128)} %bitcast.14, f32[1,512]{1,0:T(1,128)} %bitcast.15, f32[1,256]{1,0:T(1,128)} %bitcast.18, f32[1,512]{1,0:T(1,128)} %bitcast.16, f32[1,512]{1,0:T(1,128)} %bitcast.17, bf16[1024,512]{1,0:T(8,128)(2,1)} %bitcast.10, ...), custom_call_target="tpu_custom_call" | custom-call | tf_op jit(solution)/shard_map/pallas_call | solution.py:412
  52.8 1.8 %copy.13 = bf16[4,128,256]{1,0,2:T(4,128)(2,1)} copy(bf16[4,128,256]{2,1,0:T(8,128)(2,1)} %bitcast.11) | data formatting | bytes 524288 | tf_op jit(solution)/shard_map/reshape | solution.py:463

commit v5 on v4

--- a/solution.py
+++ b/solution.py
@@ -184,8 +184,6 @@
         )
         return both[:, :lanes], both[:, lanes:]
 
-    features_late.wait()
-    halo_other.start()
     load_pool.wait()
     for t in range(frames):
         one, two = pooled(wt[2 * t : 2 * t + 2])
@@ -229,16 +227,10 @@
         for kx, moved in enumerate(shifted(values.astype(BF16))):
             ref[t, inside, kx * half : (kx + 1) * half] = moved
 
-    def forward(ref, which):
-        for kt in range(3):
-            for ky in range(3):
-                left = ref[kt : kt + frames, ky * W1 : ky * W1 + CELLS, :].reshape(rows, 3 * half)
-                tap = 9 * kt + 3 * ky
-                right = jnp.concatenate([w1[tap + kx, which, :] for kx in range(3)], axis=0)
-                acc[...] += jnp.dot(left, right, preferred_element_type=F32)
-
     started = jnp.where(me > 0, 1.0, 0.0)
     mean1, inv1 = norm_of(tot1[...])
+    features_late.wait()
+    halo_other.start()
     gain1, shift1 = g1_ref[:, mine], s1_ref[:, mine]
     acc[...] = jnp.zeros_like(acc)
     for t in range(frames):
@@ -247,7 +239,6 @@
     for t in range(2):
         place(act_m, t, activate(frame(hm, t), mean1, inv1, mine) * started)
     load1.wait()
-    forward(act_m, mine)
 
     def conv_two(which):
         low[...] = jnp.zeros_like(low)
@@ -274,7 +265,21 @@
     halo_other.wait()
     for t in range(2):
         place(act_o, t, activate(frame(ho, t), mean_o, inv_o, other) * started)
-    forward(act_o, other)
+    def forward_both(kt, _):
+        for ky in range(3):
+            tap = 9 * kt + 3 * ky
+            pieces = [
+                ref[pl.ds(kt, frames), ky * W1 : ky * W1 + CELLS, :].reshape(rows, 3 * half)
+                for ref in (act_m, act_o)
+            ]
+            weights = [w1[tap + kx, which, :] for which in (mine, other) for kx in range(3)]
+            acc[...] += jnp.dot(
+                jnp.concatenate(pieces, axis=1), jnp.concatenate(weights, axis=0),
+                preferred_element_type=F32,
+            )
+        return 0
+
+    lax.fori_loop(0, 3, forward_both, 0)
     first = jnp.zeros((1, half), F32)
     second = jnp.zeros((1, half), F32)
     for t in range(frames):
@@ -365,7 +370,7 @@
     for t in range(2):
         put(frames + t, (gh[2 + t].astype(F32) * more).astype(BF16))
     back(frames - 2, 2, other)
-    exchange1.append(send_back(2 + 8, frames - 2, 2))
+    exchange1.append(send_back(10, frames - 2, 2))
 
     def slope_sums(slopes, norm_at):
         first = jnp.zeros((1, half), F32)

time: 54.9 us -> 51.7 us (0.942)
  Pallas kernels: 51 us -> 47.9 us
    pallas_call x1, Pallas kernels: 51 us -> 47.9 us  [body(): pl.pallas_call(functools.partial(kernel, n, frames), out_shape=jax.ShapeD...]
where the time goes in v5:
time: 51.7 us; the launch traced here: 51.5 us
  Pallas kernels  47.9 us (93%)
  local copies, waits for them, and re-layouts  3.63 us (7%)
    pallas_call x1, Pallas kernels, body(): pl.pallas_call(functools.partial(kernel, n, frames), out_shape=jax.ShapeD...  47.9 us
    reshape x1, local copies, waits for them, and re-layouts, body(): return jnp.transpose(out.reshape(frames, cells, half), (2, 0, 1))  1.82 us
    transpose x1, local copies, waits for them, and re-layouts, body(): across = jnp.transpose(features, (1, 2, 0)).reshape(rows, half)  1.81 us

profile of v5, /device:TPU:0, one launch (start us, length us, event | category | flops | bytes accessed | tf_op | source)
XLA Modules:
  0.0 51.5 jit_solution(2963903876208902380)
XLA Ops:
  0.0 1.8 %copy.12 = bf16[4,128,256]{2,1,0:T(8,128)(2,1)} copy(bf16[4,128,256]{1,0,2:T(4,128)(2,1)} %bitcast.13) | data formatting | bytes 524288 | tf_op jit(solution)/shard_map/transpose | solution.py:411
  1.8 47.9 %shard_map.109 = bf16[512,256]{1,0:T(8,128)(2,1)} custom-call(bf16[512,256]{1,0:T(8,128)(2,1)} %bitcast.12, s32[8]{0:T(128)} %fw_ref.1, f32[1,512]{1,0:T(1,128)} %bitcast.14, f32[1,512]{1,0:T(1,128)} %bitcast.15, f32[1,256]{1,0:T(1,128)} %bitcast.18, f32[1,512]{1,0:T(1,128)} %bitcast.16, f32[1,512]{1,0:T(1,128)} %bitcast.17, bf16[1024,512]{1,0:T(8,128)(2,1)} %bitcast.10, ...), custom_call_target="tpu_custom_call" | custom-call | tf_op jit(solution)/shard_map/pallas_call | solution.py:417
  49.7 1.8 %copy.13 = bf16[4,128,256]{1,0,2:T(4,128)(2,1)} copy(bf16[4,128,256]{2,1,0:T(8,128)(2,1)} %bitcast.11) | data formatting | bytes 524288 | tf_op jit(solution)/shard_map/reshape | solution.py:468

commit v6 on v5

--- a/solution.py
+++ b/solution.py
@@ -84,7 +84,7 @@
                 send_sem=st_send.at[index], recv_sem=st_recv.at[index],
                 device_id={"tm": lax.rem(me + k, n)}, device_id_type=MESH,
             )
-            for k in range(1, n)
+            for k in sorted(range(1, n), key=lambda k: abs(k - n // 2))
         ]
 
     def all_sums(index):

time: 51.7 us -> 52.7 us (1.019)
  Pallas kernels: 47.9 us -> 48.9 us
    pallas_call x1, Pallas kernels: 47.9 us -> 48.9 us  [body(): pl.pallas_call(functools.partial(kernel, n, frames), out_shape=jax.ShapeD...]
where the time goes in v6:
time: 52.7 us; the launch traced here: 52.5 us
  Pallas kernels  48.9 us (93%)
  local copies, waits for them, and re-layouts  3.63 us (7%)
    pallas_call x1, Pallas kernels, body(): pl.pallas_call(functools.partial(kernel, n, frames), out_shape=jax.ShapeD...  48.9 us
    reshape x1, local copies, waits for them, and re-layouts, body(): return jnp.transpose(out.reshape(frames, cells, half), (2, 0, 1))  1.82 us
    transpose x1, local copies, waits for them, and re-layouts, body(): across = jnp.transpose(features, (1, 2, 0)).reshape(rows, half)  1.81 us

profile of v6, /device:TPU:0, one launch (start us, length us, event | category | flops | bytes accessed | tf_op | source)
XLA Modules:
  0.0 52.5 jit_solution(689655882484517795)
XLA Ops:
  0.0 1.8 %copy.12 = bf16[4,128,256]{2,1,0:T(8,128)(2,1)} copy(bf16[4,128,256]{1,0,2:T(4,128)(2,1)} %bitcast.13) | data formatting | bytes 524288 | tf_op jit(solution)/shard_map/transpose | solution.py:411
  1.8 48.9 %shard_map.109 = bf16[512,256]{1,0:T(8,128)(2,1)} custom-call(bf16[512,256]{1,0:T(8,128)(2,1)} %bitcast.12, s32[8]{0:T(128)} %fw_ref.1, f32[1,512]{1,0:T(1,128)} %bitcast.14, f32[1,512]{1,0:T(1,128)} %bitcast.15, f32[1,256]{1,0:T(1,128)} %bitcast.18, f32[1,512]{1,0:T(1,128)} %bitcast.16, f32[1,512]{1,0:T(1,128)} %bitcast.17, bf16[1024,512]{1,0:T(8,128)(2,1)} %bitcast.10, ...), custom_call_target="tpu_custom_call" | custom-call | tf_op jit(solution)/shard_map/pallas_call | solution.py:417
  50.7 1.8 %copy.13 = bf16[4,128,256]{1,0,2:T(4,128)(2,1)} copy(bf16[4,128,256]{2,1,0:T(8,128)(2,1)} %bitcast.11) | data formatting | bytes 524288 | tf_op jit(solution)/shard_map/reshape | solution.py:468
